TPU v7x, 256 devices: a whole 4x4x8 slice. The times are simulated.
256 devices in a mesh: dp: 16 (over x_hi, y, core), seq: 16 (over z, x_lo).
Axes of the slice: x: 4 (x_hi: 2, x_lo: 2; x = x_hi * 2 + x_lo), y: 4, z: 8, core: 2. Of those that a mesh axis runs over, the one named last changes fastest.
Arguments:
- clip_tokens: bfloat16 [16, 16, 768, 1152], P('dp', 'seq'), may hold values from -6 to 6
- time_mod: float32 [16, 3, 1152], P('dp'), may hold values from -2 to 4
- mod_table: float32 [3, 1152], replicated, may hold values from -3 to 3
- w_qkv: bfloat16 [1152, 1728], replicated, may hold values from -0.1875 to 0.1875
- w_out: bfloat16 [576, 1152], replicated, may hold values from -0.25 to 0.25
- out_grad: bfloat16 [16, 16, 768, 1152], P('dp', 'seq'), may hold values from -6 to 6
Outputs:
- out_tokens: bfloat16 [16, 16, 768, 1152], P('dp', 'seq')
- grad_tokens: bfloat16 [16, 16, 768, 1152], P('dp', 'seq')
- grad_qkv_weight: float32 [1152, 1728], P('seq')
- grad_out_weight: float32 [576, 1152], P('seq')
- grad_table: float32 [3, 1152], replicated
All inputs are finite; a program needn't handle non-finite values.
Results may differ from a plain program's by a relative error of at most 0.0095.
The roundings to bfloat16 on the way count: a program that leaves them out, or rounds other values in their place, can miss the bound.
Values may be sent and summed in bfloat16 or wider, within the bound.
No kernel may reach another device: no remote copies, remote signals or barrier semaphores. Data moves between devices by JAX's collectives and lax.ppermute only.
A program may use at most 128 MiB of HBM per device.

v0:
```python
import math

import jax
import jax.numpy as jnp
from jax import lax
from jax.sharding import PartitionSpec as P

HEAD_DIM = 72
HEADS = 8
POS = 768
INNER = 576


EPSILON = 1e-06


def split_heads(packed):
    frames, positions = (packed.shape[0], packed.shape[1])
    return packed.reshape(frames, positions, 3, HEADS, HEAD_DIM)


def attend(packed):
    pieces = split_heads(packed)
    queries, key_rows, values = (pieces[:, :, 0], pieces[:, :, 1], pieces[:, :, 2])
    scores = jnp.einsum(
        "fmne,gmne->fmng", queries, key_rows, preferred_element_type=jnp.float32
    ) / math.sqrt(HEAD_DIM)
    row_max = jnp.max(scores, axis=3, keepdims=True)
    exp_scores = jnp.exp(scores - row_max)
    weights = exp_scores / jnp.sum(exp_scores, axis=3, keepdims=True)
    mixed = jnp.einsum(
        "fmng,gmne->fmne", weights.astype(jnp.bfloat16), values, preferred_element_type=jnp.float32
    )
    return (mixed.astype(jnp.bfloat16).reshape(packed.shape[0], packed.shape[1], INNER), weights)


def attend_grad(packed, weights, grad_mixed):
    frames, positions = (packed.shape[0], packed.shape[1])
    pieces = split_heads(packed)
    queries, key_rows, values = (pieces[:, :, 0], pieces[:, :, 1], pieces[:, :, 2])
    grad_heads = grad_mixed.reshape(frames, positions, HEADS, HEAD_DIM)
    grad_weights = jnp.einsum(
        "fmne,gmne->fmng", grad_heads, values, preferred_element_type=jnp.float32
    )
    grad_values = jnp.einsum(
        "fmng,fmne->gmne",
        weights.astype(jnp.bfloat16),
        grad_heads,
        preferred_element_type=jnp.float32,
    ).astype(jnp.bfloat16)
    row_total = jnp.sum(weights * grad_weights, axis=3, keepdims=True)
    grad_scores = (weights * (grad_weights - row_total) / math.sqrt(HEAD_DIM)).astype(jnp.bfloat16)
    grad_queries = jnp.einsum(
        "fmng,gmne->fmne", grad_scores, key_rows, preferred_element_type=jnp.float32
    ).astype(jnp.bfloat16)
    grad_keys = jnp.einsum(
        "fmng,fmne->gmne", grad_scores, queries, preferred_element_type=jnp.float32
    ).astype(jnp.bfloat16)
    stacked = jnp.stack([grad_queries, grad_keys, grad_values], axis=2)
    return stacked.reshape(frames, positions, 3 * INNER)


def body(clip_tokens, time_mod, mod_table, w_qkv, w_out, out_grad):
    modulation = mod_table + time_mod[0]
    shift_row, scale_row, gate_row = (modulation[0], modulation[1], modulation[2])
    tokens_wide = clip_tokens[0, 0].astype(jnp.float32)
    row_mean = jnp.mean(tokens_wide, axis=1, keepdims=True)
    centered = tokens_wide - row_mean
    row_var = jnp.mean(centered * centered, axis=1, keepdims=True)
    inv_std = lax.rsqrt(row_var + EPSILON)
    normed = centered * inv_std
    modulated = (normed * (1.0 + scale_row) + shift_row).astype(jnp.bfloat16)
    packed = jnp.dot(modulated, w_qkv, preferred_element_type=jnp.float32).astype(jnp.bfloat16)
    packed_pos = lax.all_to_all(packed[None], "seq", split_axis=1, concat_axis=0, tiled=True)
    mixed_pos, weights_pos = attend(packed_pos)
    mixed_here = lax.all_to_all(mixed_pos, "seq", split_axis=0, concat_axis=1, tiled=True)[0]
    branch = jnp.dot(mixed_here, w_out, preferred_element_type=jnp.float32)
    out_tokens = (tokens_wide + gate_row * branch).astype(jnp.bfloat16)
    grad_out = out_grad[0, 0].astype(jnp.float32)
    grad_gate = jnp.sum(grad_out * branch, axis=0)
    grad_branch = (grad_out * gate_row).astype(jnp.bfloat16)
    grad_wout = lax.dot_general(
        mixed_here, grad_branch, (((0,), (0,)), ((), ())), preferred_element_type=jnp.float32
    )
    grad_mixed = lax.dot_general(
        grad_branch, w_out, (((1,), (1,)), ((), ())), preferred_element_type=jnp.float32
    ).astype(jnp.bfloat16)
    grad_mixed_pos = lax.all_to_all(
        grad_mixed[None], "seq", split_axis=1, concat_axis=0, tiled=True
    )
    grad_packed_pos = attend_grad(packed_pos, weights_pos, grad_mixed_pos)
    grad_packed = lax.all_to_all(grad_packed_pos, "seq", split_axis=0, concat_axis=1, tiled=True)[0]
    grad_wqkv = lax.dot_general(
        modulated, grad_packed, (((0,), (0,)), ((), ())), preferred_element_type=jnp.float32
    )
    grad_mod = lax.dot_general(
        grad_packed, w_qkv, (((1,), (1,)), ((), ())), preferred_element_type=jnp.float32
    )
    grad_shift = jnp.sum(grad_mod, axis=0)
    grad_scale = jnp.sum(grad_mod * normed, axis=0)
    grad_normed = grad_mod * (1.0 + scale_row)
    grad_tokens = grad_out + inv_std * (
        grad_normed
        - jnp.mean(grad_normed, axis=1, keepdims=True)
        - normed * jnp.mean(grad_normed * normed, axis=1, keepdims=True)
    )
    factor = 1.0 / math.sqrt(lax.axis_size("dp") * lax.axis_size("seq") * POS)
    table_part = jnp.stack([grad_shift, grad_scale, grad_gate]) * factor
    grad_table = lax.psum(table_part, ("dp", "seq"))
    row_blocks = (
        lax.psum_scatter(grad_wqkv * factor, "seq", scatter_dimension=0, tiled=True),
        lax.psum_scatter(grad_wout * factor, "seq", scatter_dimension=0, tiled=True),
    )
    qkv_grad, out_weight_grad = lax.psum((row_blocks[0], row_blocks[1]), "dp")
    return (
        out_tokens[None, None],
        grad_tokens.astype(jnp.bfloat16)[None, None],
        qkv_grad,
        out_weight_grad,
        grad_table,
    )


def solution(mesh):
    return jax.shard_map(
        body,
        mesh=mesh,
        in_specs=(
            P("dp", "seq", None, None),
            P("dp", None, None),
            P(),
            P(),
            P(),
            P("dp", "seq", None, None),
        ),
        out_specs=(
            P("dp", "seq", None, None),
            P("dp", "seq", None, None),
            P("seq", None),
            P("seq", None),
            P(),
        ),
        check_vma=False,
    )
```

profile of v0, /device:TPU:1, one launch (start us, length us, event | category | flops | bytes accessed | tf_op | source)
XLA Modules:
  0.0 744.3 jit_solution(15065676621597504609)
XLA Ops:
  7.2 0.0 copy-start
  7.2 0.8 bitcast_add_fusion
  8.1 0.0 copy-start.10
  8.1 0.4 copy-done
  8.5 3.7 fusion.71
  12.3 3.8 copy.35
  16.0 0.5 broadcast.92
  16.5 7.9 %reduce.11 = bf16[768,576]{1,0:T(8,128)(2,1)} reduce(bf16[768,1,576]{2,1,0:T(2,128)(2,1)S(1)} %bitcast.161, bf16[]{:T(256)} %broadcast.92), dimensions={1}, to_apply=%bitcast.146.reduce_sub_computation | reduce | bytes 1769474
  24.4 3.7 reshape.112
  28.2 10.3 %all-to-all-start.2 = ((bf16[16,2,13824]{2,1,0:T(2,128)(2,1)}), bf16[16,2,13824]{2,1,0:T(2,128)(2,1)}, u32[]{:S(2)}, u32[]{:S(2)}) async-start(bf16[16,2,13824]{2,1,0:T(2,128)(2,1)} %reshape.112), calls=%async_computation.2 | async-start | bytes 1769472 | tf_op jit(solution)/shard_map/all_to_all | solution.py:88
  38.5 0.3 convert_reduce_fusion
  38.8 0.6 fusion.20
  39.4 7.5 %fusion.35 = bf16[1,768,1728]{1,2,0:T(8,128)(2,1)} fusion(bf16[1152,1728]{0,1:T(8,128)(2,1)} %param.9, bf16[1,1,768,1152]{3,2,1,0:T(8,128)(2,1)S(1)} %copy-done.1, f32[1152]{0:T(1024)S(1)} %get-tuple-element.10, f32[1152]{0:T(1024)S(1)} %get-tuple-element.11, f32[768]{0:T(1024)S(1)} %add_rsqrt_fusion, f32[768]{0:T(1024)S(1)} %broadcast_multiply_fusion.2), kind=kOutput, calls=%fused_computation.48 | convolution fusion | flops 3064283136 | bytes 8420352 | tf_op jit(solution)/shard_map/dot_general | solution.py:73
  46.9 12.6 %copy.29 = bf16[1,768,1728]{2,0,1:T(2,128)(2,1)} copy(bf16[1,768,1728]{1,2,0:T(8,128)(2,1)} %fusion.35) | data formatting | bytes 5308416 | tf_op jit(solution)/shard_map/broadcast_in_dim | solution.py:74
  59.5 18.9 %reduce.12 = bf16[768,1728]{1,0:T(8,128)(2,1)} reduce(bf16[768,1,1728]{2,1,0:T(2,128)(2,1)} %bitcast.160, bf16[]{:T(256)} %broadcast.92), dimensions={1}, to_apply=%bitcast.144.reduce_sub_computation | reduce | bytes 5308418
  78.4 7.6 %reshape.110 = bf16[16,2,41472]{2,1,0:T(2,128)(2,1)} reshape(bf16[768,1728]{1,0:T(8,128)(2,1)} %reduce.12) | data formatting | bytes 5308416
  86.0 7.7 %all-to-all-start = ((bf16[16,2,41472]{2,1,0:T(2,128)(2,1)}), bf16[16,2,41472]{2,1,0:T(2,128)(2,1)}, u32[]{:S(2)}, u32[]{:S(2)}) async-start(bf16[16,2,41472]{2,1,0:T(2,128)(2,1)} %reshape.110), calls=%async_computation | async-start | bytes 5308416 | tf_op jit(solution)/shard_map/all_to_all | solution.py:74
  93.7 0.4 reduce-scatter.4.cloned.1.call-start
  94.2 4.7 reshape.113
  98.9 6.5 bitcast_reduce_fusion.2
  105.4 3.8 reshape.101
  109.3 44.9 %all-to-all-done = bf16[16,2,41472]{2,1,0:T(2,128)(2,1)} async-done(((bf16[16,2,41472]{2,1,0:T(2,128)(2,1)}), bf16[16,2,41472]{2,1,0:T(2,128)(2,1)}, u32[]{:S(2)}, u32[]{:S(2)}) %all-to-all-start) | async-done | bytes 2654240 | tf_op jit(solution)/shard_map/all_to_all | solution.py:74
  154.2 12.1 %reshape.111 = bf16[768,1,1728]{2,1,0:T(2,128)(2,1)} reshape(bf16[16,2,41472]{2,1,0:T(2,128)(2,1)} %all-to-all-done) | data formatting | bytes 5308416
  166.3 19.0 %bitcast_reduce_fusion.1 = bf16[768,1728]{1,0:T(8,128)(2,1)} fusion(bf16[768,1,1728]{2,1,0:T(2,128)(2,1)} %reshape.111), kind=kLoop, calls=%fused_computation.105 | loop fusion | bytes 5308416 | tf_op jit(solution)/shard_map/all_to_all | solution.py:74
  185.3 8.9 %reshape.99 = bf16[16,48,3,8,72]{4,3,2,1,0:T(8,128)(2,1)} reshape(bf16[768,1728]{1,0:T(8,128)(2,1)} %bitcast_reduce_fusion.1) | data formatting | bytes 5308416 | tf_op jit(solution)/shard_map/reshape | solution.py:19
  194.3 2.8 fusion.82
  197.1 1.9 fusion.67
  199.0 2.9 fusion.83
  201.9 3.5 fusion.66
  205.4 8.7 %fusion.60 = bf16[16,48,1,8,72]{4,0,3,1,2:T(8,128)(2,1)} fusion(bf16[16,48,1,8,72]{4,3,2,1,0:T(8,128)(2,1)} %copy-done.4, f32[48,8,16,16]{3,2,1,0:T(8,128)} %fusion.66, f32[16,48,8,16]{0,3,2,1:T(8,128)} %get-tuple-element.21, f32[16,48,8]{0,2,1:T(8,128)S(1)} %get-tuple-element.20), kind=kOutput, calls=%fused_computation.75 | convolution fusion | flops 15292431 | bytes 2580480 | tf_op jit(solution)/shard_map/fmng,gmne->fmne/dot_general | solution.py:53
  214.1 8.1 %fusion.61 = bf16[16,48,1,8,72]{4,0,3,1,2:T(8,128)(2,1)} fusion(bf16[16,48,1,8,72]{4,3,2,1,0:T(8,128)(2,1)S(1)} %get-tuple-element.14, f32[48,8,16,16]{3,2,1,0:T(8,128)} %fusion.66, f32[16,48,8,16]{0,3,2,1:T(8,128)} %get-tuple-element.21, f32[16,48,8]{0,2,1:T(8,128)S(1)} %get-tuple-element.20), kind=kOutput, calls=%fused_computation.76 | convolution fusion | flops 15292431 | bytes 2580480 | tf_op jit(solution)/shard_map/fmng,fmne->gmne/dot_general | solution.py:56
  222.2 3.7 fusion.62
  225.9 1.4 pad_maximum_fusion
  227.3 3.3 copy.39
  230.6 7.9 %reshape.102 = bf16[16,48,1728]{2,1,0:T(8,128)(2,1)} reshape(bf16[16,48,3,8,72]{4,3,2,1,0:T(8,128)(2,1)} %copy.39) | data formatting | bytes 5308416 | tf_op jit(solution)/shard_map/reshape | solution.py:60
  238.5 70.3 %all_to_all.16 = bf16[16,48,1728]{2,1,0:T(8,128)(2,1)S(1)} all-to-all(bf16[16,48,1728]{2,1,0:T(8,128)(2,1)} %reshape.102), channel_id=1, replica_groups=mesh['dp'=16,'seq'=16] {'seq'}, dimensions={0} | all-to-all | bytes 5308416 | tf_op jit(solution)/shard_map/all_to_all | solution.py:92
  308.8 1.6 copy-done.6
  310.4 6.5 convolution_multiply_fusion
  316.9 0.0 reduce-scatter.4.cloned.1.call-update
  316.9 0.0 all-reduce.5.cloned.1.call-start
  316.9 3.6 fusion.59
  320.5 1.6 copy.34
  322.1 3.7 reshape.100
  325.8 37.2 %all_to_all.17 = bf16[16,48,576]{2,1,0:T(8,128)(2,1)S(1)} all-to-all(bf16[16,48,576]{2,1,0:T(8,128)(2,1)} %reshape.100), channel_id=1, replica_groups=mesh['dp'=16,'seq'=16] {'seq'}, dimensions={0} | all-to-all | bytes 1769472 | tf_op jit(solution)/shard_map/all_to_all | solution.py:76
  362.9 0.9 copy-done.9
  363.9 4.4 convolution_multiply_fusion.1
  368.3 150.7 %fusion = f32[48,1152]{1,0:T(8,128)S(1)} fusion(f32[576,1152]{1,0:T(8,128)} %convolution_multiply_fusion.1), kind=kCustom, calls=%all-reduce-scatter | all-reduce-scatter fusion | flops 884737 | bytes 2876416
  519.0 1.8 collective-permute-start
  520.8 3.8 collective-permute-start.1
  524.7 6.0 collective-permute-start.2
  530.7 0.7 slice.33
  531.4 6.4 collective-permute-start.3
  537.8 1.3 dynamic-slice.4
  539.7 0.3 collective-permute-done.3
  540.0 8.3 %concatenate = f32[228,1152]{1,0:T(8,128)} concatenate(f32[36,1152]{1,0:T(8,128)} %collective-permute-done.3, f32[48,1152]{1,0:T(8,128)} %collective-permute-done.2, f32[48,1152]{1,0:T(8,128)} %collective-permute-done.1, f32[48,1152]{1,0:T(8,128)S(1)} %collective-permute-done, f32[48,1152]{1,0:T(8,128)S(1)} %fusion), dimensions={0} | concatenate | bytes 2101248
  548.3 1.6 constant_dynamic-slice_fusion
  549.9 8.7 %fusion.19 = (f32[1152]{0:T(1024)S(1)}, f32[768]{0:T(1024)S(1)}, f32[768]{0:T(1024)S(1)}, f32[1152]{0:T(1024)S(1)}, f32[768,1152]{1,0:T(8,128)}) fusion(bf16[1,1,768,1152]{3,2,1,0:T(8,128)(2,1)S(1)} %copy-done.2, f32[768]{0:T(1024)S(1)} %add_rsqrt_fusion, f32[768]{0:T(1024)S(1)} %broadcast_multiply_fusion.2, f32[1152]{0:T(1024)} %copy-done.10, ...), kind=kOutput, calls=%fused_computation.26 | convolution fusion | flops 3066491392 | bytes 11970048 | tf_op jit(solution)/shard_map/dot_general | solution.py:96
  558.6 28.3 %reduce-scatter.4.cloned.1.call-done = f32[72,1728]{1,0:T(8,128)} async-done(((f32[1152,1728]{1,0:T(8,128)}), f32[72,1728]{1,0:T(8,128)}) %reduce-scatter.4.cloned.1.call-update) | async-done | bytes 497680 | tf_op jit(solution)/shard_map/reduce_scatter | solution.py:111
  586.9 0.0 all-reduce.5.cloned.1.call-update
  586.9 7.3 fusion.23
  594.3 78.0 %psum.23 = f32[3,1152]{1,0:T(4,128)} all-reduce(f32[3,1152]{1,0:T(4,128)S(1)} %maximum_multiply_fusion), channel_id=1, replica_groups=mesh['dp'=16,'seq'=16] {'dp','seq'}, use_global_device_ids=true, to_apply=%region_14.0 | all-reduce | flops 3456 | bytes 27648 | tf_op jit(solution)/shard_map/psum | solution.py:109
  672.3 61.3 %all-reduce.5.cloned.1.call-done = (f32[72,1728]{1,0:T(8,128)}, f32[36,1152]{1,0:T(8,128)}) async-done(((f32[72,1728]{1,0:T(8,128)}, f32[36,1152]{1,0:T(8,128)}), (f32[72,1728]{1,0:T(8,128)}, f32[36,1152]{1,0:T(8,128)})) %all-reduce.5.cloned.1.call-update) | async-done | bytes 663568 | tf_op jit(solution)/shard_map/psum | solution.py:114
  733.6 1.9 copy.62
  735.5 1.6 copy.63
  (31 shorter events, 0.1 us)
Async XLA Ops:
  7.2 1.4 copy-start
  8.1 300.7 %copy-start.10 = (f32[1152]{0:T(1024)}, f32[1152]{0:T(1024)S(1)}, u32[]{:S(2)}) copy-start(f32[1152]{0:T(1024)S(1)} %get-tuple-element.11) | copy-start | bytes 13828
  24.4 14.1 %copy-start.1 = (bf16[1,1,768,1152]{3,2,1,0:T(8,128)(2,1)S(1)}, bf16[1,1,768,1152]{3,2,1,0:T(8,128)(2,1)}, u32[]{:S(2)}) copy-start(bf16[1,1,768,1152]{3,2,1,0:T(8,128)(2,1)} %param.6) | copy-start | bytes 5308420
  28.2 57.8 %all-to-all-start.2 = ((bf16[16,2,13824]{2,1,0:T(2,128)(2,1)}), bf16[16,2,13824]{2,1,0:T(2,128)(2,1)}, u32[]{:S(2)}, u32[]{:S(2)}) async-start(bf16[16,2,13824]{2,1,0:T(2,128)(2,1)} %reshape.112), calls=%async_computation.2 | async-start | bytes 1769472 | tf_op jit(solution)/shard_map/all_to_all | solution.py:88
  86.0 68.2 %all-to-all-start = ((bf16[16,2,41472]{2,1,0:T(2,128)(2,1)}), bf16[16,2,41472]{2,1,0:T(2,128)(2,1)}, u32[]{:S(2)}, u32[]{:S(2)}) async-start(bf16[16,2,41472]{2,1,0:T(2,128)(2,1)} %reshape.110), calls=%async_computation | async-start | bytes 5308416 | tf_op jit(solution)/shard_map/all_to_all | solution.py:74
  93.7 493.1 %reduce-scatter.4.cloned.1.call-start = ((), (), s32[]{:S(2)}) async-start(), calls=%async_computation.5 | async-start | bytes 8773632 | tf_op jit(solution)/shard_map/reduce_scatter | solution.py:111
  197.1 1.9 copy-start.4
  197.1 4.8 copy-start.3
  199.0 2.9 copy-start.5
  222.2 3.7 copy-start.7
  222.2 3.7 copy-start.8
  238.5 71.9 %copy-start.2 = (bf16[1,1,768,1152]{3,2,1,0:T(8,128)(2,1)S(1)}, bf16[1,1,768,1152]{3,2,1,0:T(8,128)(2,1)}, u32[]{:S(2)}) copy-start(bf16[1,1,768,1152]{3,2,1,0:T(8,128)(2,1)} %param.6) | copy-start | bytes 5308420
  308.8 1.6 copy-start.6
  316.9 416.7 %all-reduce.5.cloned.1.call-start = ((), (), s32[]{:S(2)}) async-start(), calls=%async_computation.6 | async-start | bytes 1400832 | tf_op jit(solution)/shard_map/psum | solution.py:114
  362.9 1.0 copy-start.9
  519.0 21.0 %collective-permute-start = (f32[48,1152]{1,0:T(8,128)S(1)}, f32[48,1152]{1,0:T(8,128)S(1)}, u32[]{:S(2)}, u32[]{:S(2)}) collective-permute-start(f32[48,1152]{1,0:T(8,128)S(1)} %fusion), channel_id=1, source_target_pairs={{0,1},{1,2},{2,3},{3,4},{4,5},{5,6},{6,7},{7,8},{8,9},{9,10},{10,1... | collective-permute-start | bytes 663560
  520.8 19.2 %collective-permute-start.1 = (f32[48,1152]{1,0:T(8,128)S(1)}, f32[48,1152]{1,0:T(8,128)}, u32[]{:S(2)}, u32[]{:S(2)}) collective-permute-start(f32[48,1152]{1,0:T(8,128)S(1)} %fusion), channel_id=1, source_target_pairs={{0,2},{1,3},{2,4},{3,5},{4,6},{5,7},{6,8},{7,9},{8,10},{9,11},{10,... | collective-permute-start | bytes 663560
  524.7 15.3 %collective-permute-start.2 = (f32[48,1152]{1,0:T(8,128)S(1)}, f32[48,1152]{1,0:T(8,128)}, u32[]{:S(2)}, u32[]{:S(2)}) collective-permute-start(f32[48,1152]{1,0:T(8,128)S(1)} %fusion), channel_id=1, source_target_pairs={{0,3},{1,4},{2,5},{3,6},{4,7},{5,8},{6,9},{7,10},{8,11},{9,12},{10... | collective-permute-start | bytes 663560
  531.4 8.6 %collective-permute-start.3 = (f32[36,1152]{1,0:T(8,128)}, f32[36,1152]{1,0:T(8,128)}, u32[]{:S(2)}, u32[]{:S(2)}) collective-permute-start(f32[36,1152]{1,0:T(8,128)} %slice.33), channel_id=1, source_target_pairs={{0,4},{1,5},{2,6},{3,7},{4,8},{5,9},{6,10},{7,11},{8,12},{9,13},{1... | collective-permute-start | bytes 497672
  549.9 37.0 %copy-start.11 = (f32[1152]{0:T(1024)S(1)}, f32[1152]{0:T(1024)}, u32[]{:S(2)}) copy-start(f32[1152]{0:T(1024)} %copy-done.10) | copy-start | bytes 13828
Sparse Core Ops, SparseCore 0:
  317.0 269.8 reduce-scatter.3
  590.3 143.2 all-reduce.4
where the time goes:
time: 756 us; the launch traced here: 744 us
  blocking collectives  336 us (44%)
  waiting for transfers between devices  135 us (18%)
  local copies, waits for them, and re-layouts  121 us (16%)
  matrix products  67.5 us (9%)
  starting transfers between devices  36.5 us (5%)
  other arithmetic  32.9 us (4%)
  between operations  15.4 us (2%)
    unnamed x1, blocking collectives  151 us
    psum x1, blocking collectives, body(): grad_table = lax.psum(table_part, ('dp', 'seq'))  78 us
    all_to_all x1, blocking collectives, body(): lax.all_to_all(grad_packed_pos, 'seq', split_axis=0, concat_axis=1, tiled...  70.3 us
    psum x1, waiting for transfers between devices, body(): qkv_grad, out_weight_grad = lax.psum((row_blocks[0], row_blocks[1]), 'dp')  61.3 us
    unnamed x35, local copies, waits for them, and re-layouts  47 us
    all_to_all x1, waiting for transfers between devices, body(): lax.all_to_all(packed[None], 'seq', split_axis=1, concat_axis=0, tiled=True)  44.9 us
    all_to_all x1, blocking collectives, body(): lax.all_to_all(mixed_pos, 'seq', split_axis=0, concat_axis=1, tiled=True)[0]  37.2 us
    reduce_scatter x1, waiting for transfers between devices, body(): lax.psum_scatter(grad_wqkv * factor, 'seq', scatter_dimension=0, tiled=True)  28.3 us
  transfers between devices with their start and end apart: 8, of which 4 were waited for; matrix products, arithmetic and copies ran while one was open for 34% of the time, Pallas kernels for 0%

commit v1 on v0

v1 whole, which is shorter than its diff:
```python
import functools
import math

import jax
import jax.numpy as jnp
from jax import lax
from jax.experimental import pallas as pl
from jax.experimental.pallas import tpu as pltpu
from jax.sharding import PartitionSpec as P

D = 1152
HEAD_DIM = 72
HEADS = 8
POS = 768
INNER = 576
SEQ = 16
DP = 16
HERE = POS // SEQ
TILE = 16
ROWS = SEQ * TILE
STEPS = HERE // TILE
EPSILON = 1e-06
SCALE = 1.0 / math.sqrt(HEAD_DIM)
BF = jnp.bfloat16
F32 = jnp.float32
PARAMS = pltpu.CompilerParams(
    dimension_semantics=("arbitrary",), vmem_limit_bytes=56 * 1024 * 1024
)
NT = (((1,), (1,)), ((), ()))
TN = (((0,), (0,)), ((), ()))


def dot(a, b, dims=(((1,), (0,)), ((), ()))):
    return lax.dot_general(a, b, dims, preferred_element_type=F32)


def normalize(x):
    centered = x - jnp.mean(x, axis=1, keepdims=True)
    inv_std = lax.rsqrt(jnp.mean(centered * centered, axis=1, keepdims=True) + EPSILON)
    return centered * inv_std, inv_std


def position_mask():
    rows = lax.broadcasted_iota(jnp.int32, (ROWS, ROWS), 0) % TILE
    cols = lax.broadcasted_iota(jnp.int32, (ROWS, ROWS), 1) % TILE
    return jnp.where(rows == cols, 0.0, -1e30).astype(F32)


def softmax(queries, key_rows, mask):
    scores = dot(queries, key_rows, NT) * SCALE + mask
    exp_scores = jnp.exp(scores - jnp.max(scores, axis=1, keepdims=True))
    return exp_scores * (1.0 / jnp.sum(exp_scores, axis=1, keepdims=True))


def head(array, part, n):
    start = part * INNER + n * HEAD_DIM
    return array[:, start : start + HEAD_DIM]


def forward_kernel(x_ref, mod_ref, w_ref, packed_ref, mixed_ref):
    normed, _ = normalize(x_ref[...].reshape(ROWS, D).astype(F32))
    modulated = (normed * (1.0 + mod_ref[1:2, :]) + mod_ref[0:1, :]).astype(BF)
    packed = dot(modulated, w_ref[...]).astype(BF)
    packed_ref[...] = packed.reshape(SEQ, TILE, 3 * INNER)
    mask = position_mask()
    pieces = []
    for n in range(HEADS):
        weights = softmax(head(packed, 0, n), head(packed, 1, n), mask)
        pieces.append(dot(weights.astype(BF), head(packed, 2, n)).astype(BF))
    mixed_ref[...] = jnp.concatenate(pieces, axis=1).reshape(SEQ, TILE, INNER)


def forward(x, modulation, w_qkv):
    return pl.pallas_call(
        forward_kernel,
        grid=(STEPS,),
        in_specs=[
            pl.BlockSpec((SEQ, TILE, D), lambda j: (0, j, 0)),
            pl.BlockSpec((3, D), lambda j: (0, 0)),
            pl.BlockSpec((D, 3 * INNER), lambda j: (0, 0)),
        ],
        out_specs=[
            pl.BlockSpec((SEQ, TILE, 3 * INNER), lambda j: (0, j, 0)),
            pl.BlockSpec((SEQ, TILE, INNER), lambda j: (0, j, 0)),
        ],
        out_shape=[
            jax.ShapeDtypeStruct((SEQ, HERE, 3 * INNER), BF),
            jax.ShapeDtypeStruct((SEQ, HERE, INNER), BF),
        ],
        compiler_params=PARAMS,
        cost_estimate=pl.CostEstimate(
            flops=2 * POS * D * 3 * INNER * 3, bytes_accessed=12_000_000, transcendentals=1_600_000
        ),
        name="forward",
    )(x, modulation, w_qkv)


def backward_kernel(
    core_ref, x_ref, packed_ref, gm_ref, mod_ref, w_ref,
    delta_ref, keep_ref, send_ref, table_ref,
    modulated_all, gp_all, total,
):
    step = pl.program_id(0)
    normed, inv_std = normalize(x_ref[...].reshape(ROWS, D).astype(F32))
    scale_row = 1.0 + mod_ref[1:2, :]
    modulated_all[pl.ds(step * ROWS, ROWS), :] = (normed * scale_row + mod_ref[0:1, :]).astype(BF)
    packed = packed_ref[...].reshape(ROWS, 3 * INNER)
    grad_mixed = gm_ref[...].reshape(ROWS, INNER)
    mask = position_mask()
    pieces = [[], [], []]
    for n in range(HEADS):
        queries, key_rows, values = (head(packed, part, n) for part in range(3))
        weights = softmax(queries, key_rows, mask)
        grad_head = head(grad_mixed, 0, n)
        grad_weights = dot(grad_head, values, NT)
        row_total = jnp.sum(weights * grad_weights, axis=1, keepdims=True)
        grad_scores = (weights * (grad_weights - row_total) * SCALE).astype(BF)
        pieces[0].append(dot(grad_scores, key_rows).astype(BF))
        pieces[1].append(dot(grad_scores, queries, TN).astype(BF))
        pieces[2].append(dot(weights.astype(BF), grad_head, TN).astype(BF))
    grad_packed = jnp.concatenate(pieces[0] + pieces[1] + pieces[2], axis=1)
    gp_all[pl.ds(step * ROWS, ROWS), :] = grad_packed
    grad_mod = dot(grad_packed, w_ref[...], NT)
    shift_sum = jnp.sum(grad_mod, axis=0, keepdims=True)
    scale_sum = jnp.sum(grad_mod * normed, axis=0, keepdims=True)
    grad_normed = grad_mod * scale_row
    delta = inv_std * (
        grad_normed
        - jnp.mean(grad_normed, axis=1, keepdims=True)
        - normed * jnp.mean(grad_normed * normed, axis=1, keepdims=True)
    )
    delta_ref[...] = delta.astype(BF).reshape(SEQ, TILE, D)

    @pl.when(step == 0)
    def _():
        table_ref[...] = jnp.zeros_like(table_ref)

    table_ref[0:1, :] += shift_sum
    table_ref[1:2, :] += scale_sum

    @pl.when(step == STEPS - 1)
    def _():
        for r in range(3):
            part = slice(r * 384, r * 384 + 384)
            total[part, :] = dot(modulated_all[:, part], gp_all[...], TN)
        core = core_ref[0]
        rows = D // DP
        for k in range(DP // 2):
            mine = pl.multiple_of((2 * k + core) * rows, 8)
            other = pl.multiple_of((2 * k + 1 - core) * rows, 8)
            keep_ref[k] = total[pl.ds(mine, rows), :].astype(BF)
            send_ref[k] = total[pl.ds(other, rows), :].astype(BF)


def backward(core, x, packed, grad_mixed, modulation, w_qkv):
    rows = D // DP
    half = jax.ShapeDtypeStruct((DP // 2, rows, 3 * INNER), BF)
    return pl.pallas_call(
        backward_kernel,
        grid=(STEPS,),
        in_specs=[
            pl.BlockSpec(memory_space=pltpu.SMEM),
            pl.BlockSpec((SEQ, TILE, D), lambda j: (0, j, 0)),
            pl.BlockSpec((SEQ, TILE, 3 * INNER), lambda j: (0, j, 0)),
            pl.BlockSpec((SEQ, TILE, INNER), lambda j: (0, j, 0)),
            pl.BlockSpec((3, D), lambda j: (0, 0)),
            pl.BlockSpec((D, 3 * INNER), lambda j: (0, 0)),
        ],
        out_specs=[
            pl.BlockSpec((SEQ, TILE, D), lambda j: (0, j, 0)),
            pl.BlockSpec(half.shape, lambda j: (0, 0, 0)),
            pl.BlockSpec(half.shape, lambda j: (0, 0, 0)),
            pl.BlockSpec((8, D), lambda j: (0, 0)),
        ],
        out_shape=[
            jax.ShapeDtypeStruct((SEQ, HERE, D), BF),
            half,
            half,
            jax.ShapeDtypeStruct((8, D), F32),
        ],
        scratch_shapes=[
            pltpu.VMEM((POS, D), BF),
            pltpu.VMEM((POS, 3 * INNER), BF),
            pltpu.VMEM((D, 3 * INNER), F32),
        ],
        compiler_params=PARAMS,
        cost_estimate=pl.CostEstimate(
            flops=2 * POS * D * 3 * INNER * 5, bytes_accessed=20_000_000, transcendentals=1_600_000
        ),
        name="backward",
    )(core, x, packed, grad_mixed, modulation, w_qkv)


def output_kernel(
    core_ref, mixed_ref, x_ref, grad_ref, mod_ref, w_ref, out_ref, keep_ref, send_ref, gate_ref, total
):
    step = pl.program_id(0)
    gate_row = mod_ref[2:3, :]
    mixed = mixed_ref[...]
    branch = dot(mixed, w_ref[...])
    out_ref[...] = (x_ref[...].astype(F32) + gate_row * branch).astype(BF)
    grad_out = grad_ref[...].astype(F32)
    gate_sum = jnp.sum(grad_out * branch, axis=0, keepdims=True)
    term = dot(mixed, (grad_out * gate_row).astype(BF), TN)

    @pl.when(step == 0)
    def _():
        total[...] = jnp.zeros_like(total)
        gate_ref[...] = jnp.zeros_like(gate_ref)

    total[...] += term
    gate_ref[0:1, :] += gate_sum

    @pl.when(step == POS // ROWS - 1)
    def _():
        rows = INNER // DP
        core = core_ref[0]
        for k in range(DP // 2):
            both = total[2 * k * rows : 2 * (k + 1) * rows, :]
            first, second = both[:rows].astype(BF), both[rows:].astype(BF)
            keep_ref[k] = jnp.where(core == 0, first, second)
            send_ref[k] = jnp.where(core == 0, second, first)


def output(core, mixed, x, out_grad, modulation, w_out):
    half = jax.ShapeDtypeStruct((DP // 2, INNER // DP, D), BF)
    return pl.pallas_call(
        output_kernel,
        grid=(POS // ROWS,),
        in_specs=[
            pl.BlockSpec(memory_space=pltpu.SMEM),
            pl.BlockSpec((ROWS, INNER), lambda j: (j, 0)),
            pl.BlockSpec((ROWS, D), lambda j: (j, 0)),
            pl.BlockSpec((ROWS, D), lambda j: (j, 0)),
            pl.BlockSpec((3, D), lambda j: (0, 0)),
            pl.BlockSpec((INNER, D), lambda j: (0, 0)),
        ],
        out_specs=[
            pl.BlockSpec((ROWS, D), lambda j: (j, 0)),
            pl.BlockSpec(half.shape, lambda j: (0, 0, 0)),
            pl.BlockSpec(half.shape, lambda j: (0, 0, 0)),
            pl.BlockSpec((8, D), lambda j: (0, 0)),
        ],
        out_shape=[
            jax.ShapeDtypeStruct((POS, D), BF),
            half,
            half,
            jax.ShapeDtypeStruct((8, D), F32),
        ],
        scratch_shapes=[pltpu.VMEM((INNER, D), F32)],
        compiler_params=PARAMS,
        cost_estimate=pl.CostEstimate(
            flops=4 * POS * D * INNER, bytes_accessed=9_000_000, transcendentals=0
        ),
        name="output",
    )(core, mixed, x, out_grad, modulation, w_out)


def exchange(blocks, axis, groups=None):
    return lax.all_to_all(blocks, axis, 0, 0, axis_index_groups=groups, tiled=True)


def wide_sum(blocks):
    return jnp.sum(blocks.astype(F32), axis=0)


def body(clip_tokens, time_mod, mod_table, w_qkv, w_out, out_grad):
    tokens, grad_rows = clip_tokens[0, 0], out_grad[0, 0]
    modulation = mod_table + time_mod[0]
    core = lax.rem(lax.axis_index("dp"), 2).astype(jnp.int32).reshape(1)
    x_pos = exchange(tokens.reshape(SEQ, HERE, D), "seq")
    grad_branch = (grad_rows.astype(F32) * modulation[2]).astype(BF)
    grad_mixed = dot(grad_branch, w_out, NT).astype(BF)
    gm_pos = exchange(grad_mixed.reshape(SEQ, HERE, INNER), "seq")
    packed, mixed_pos = forward(x_pos, modulation, w_qkv)
    mixed = exchange(mixed_pos, "seq").reshape(POS, INNER)
    delta_pos, qkv_keep, qkv_send, table2 = backward(core, x_pos, packed, gm_pos, modulation, w_qkv)
    delta = exchange(delta_pos, "seq").reshape(POS, D)
    out_tokens, out_keep, out_send, gate_sum = output(
        core, mixed, tokens, grad_rows, modulation, w_out
    )
    grad_tokens = (grad_rows.astype(F32) + delta.astype(F32)).astype(BF)

    factor = 1.0 / math.sqrt(DP * SEQ * POS)
    swap = [(i, i ^ 1) for i in range(DP)]
    chips = [[2 * k + c for k in range(DP // 2)] for c in range(2)]
    table = jnp.concatenate([table2[0:2], gate_sum[0:1]], axis=0)

    def over_dp(keep, send):
        pair = keep.astype(F32) + lax.ppermute(send, "dp", swap).astype(F32)
        return wide_sum(exchange(pair.astype(BF), "dp", chips))

    qkv_block = over_dp(qkv_keep, qkv_send)
    out_block = over_dp(out_keep, out_send)
    table = table + lax.ppermute(table, "dp", swap)
    table = wide_sum(exchange(jnp.broadcast_to(table[None], (DP // 2, 3, D)), "dp", chips))

    def pieces(block, n):
        return jnp.moveaxis(block.reshape(block.shape[0], SEQ, n), 1, 0)

    small = jnp.concatenate(
        [
            jnp.pad(pieces(qkv_block, 108), ((0, 0), (0, 0), (0, 20))),
            jnp.pad(pieces(out_block, 72), ((0, 0), (0, 4), (0, 56))),
        ],
        axis=1,
    ).astype(BF)
    small = wide_sum(exchange(small, "seq")) * factor
    table = wide_sum(exchange(jnp.broadcast_to(table[None], (SEQ, 3, D)), "seq")) * factor
    turn = [(i * SEQ + s, s * SEQ + i) for i in range(DP) for s in range(SEQ)]
    small = lax.ppermute(small, ("dp", "seq"), turn)
    small = exchange(jnp.broadcast_to(small[None], (DP,) + small.shape), "dp")
    qkv_grad = jnp.moveaxis(small[:, :72, :108], 0, 1).reshape(72, 3 * INNER)
    out_weight_grad = jnp.moveaxis(small[:, 72:108, :72], 0, 1).reshape(36, D)
    return (
        out_tokens[None, None],
        grad_tokens[None, None],
        qkv_grad,
        out_weight_grad,
        table,
    )


def solution(mesh):
    return jax.shard_map(
        body,
        mesh=mesh,
        in_specs=(
            P("dp", "seq", None, None),
            P("dp", None, None),
            P(),
            P(),
            P(),
            P("dp", "seq", None, None),
        ),
        out_specs=(
            P("dp", "seq", None, None),
            P("dp", "seq", None, None),
            P("seq", None),
            P("seq", None),
            P(),
        ),
        check_vma=False,
    )
```

time: 756 us -> 308 us (0.41); the launches traced: 744 us -> 307 us
  blocking collectives: 336 us -> 16.3 us
  local copies, waits for them, and re-layouts: 121 us -> 18.6 us
  matrix products: 67.5 us -> 3.6 us
  Pallas kernels: 0 us -> 50.2 us
  starting transfers between devices: 36.5 us -> 74.1 us
  other arithmetic: 32.9 us -> 10.4 us
  between operations: 15.4 us -> 0.89 us
    unnamed x1 -> x0, blocking collectives: 151 us -> none
    all_to_all x2 -> x1, blocking collectives: 107 us -> 16.3 us  [exchange(): lax.all_to_all(blocks, axis, 0, 0, axis_index_groups=groups, tiled=True)]
    all_to_all x2 -> x9, waiting for transfers between devices: 44.9 us -> 131 us  [exchange(): lax.all_to_all(blocks, axis, 0, 0, axis_index_groups=groups, tiled=True)]
    psum x1 -> x0, blocking collectives: 78 us -> none  [body(): grad_table = lax.psum(table_part, ('dp', 'seq'))]
    dot_general x12 -> x1, matrix products: 67.5 us -> 3.6 us  [dot(): return lax.dot_general(a, b, dims, preferred_element_type=F32)]
    psum x1 -> x0, waiting for transfers between devices: 61.3 us -> none  [body(): qkv_grad, out_weight_grad = lax.psum((row_blocks[0], row_blocks[1]), 'dp')]
    pallas_call x0 -> x3, Pallas kernels: none -> 50.2 us  [the longest x1 28.9 us: backward(): pl.pallas_call(backward_kernel, grid=(STEPS,), in_specs=[pl.BlockSpec(mem...]
    all_to_all x2 -> x9, starting transfers between devices: 18 us -> 64.7 us  [exchange(): lax.all_to_all(blocks, axis, 0, 0, axis_index_groups=groups, tiled=True)]
  transfers between devices with their start and end apart: 8 -> 13, of which waited for: 4 -> 9; matrix products, arithmetic and copies ran while one was open for 34% -> 9% of each run, Pallas kernels for 0% -> 16%
where the time goes in v1:
time: 308 us; the launch traced here: 307 us
  waiting for transfers between devices  133 us (43%)
  starting transfers between devices  74.1 us (24%)
  Pallas kernels  50.2 us (16%)
  local copies, waits for them, and re-layouts  18.6 us (6%)
  blocking collectives  16.3 us (5%)
  other arithmetic  10.4 us (3%)
  matrix products  3.6 us (1%)
    all_to_all x9, waiting for transfers between devices, exchange(): lax.all_to_all(blocks, axis, 0, 0, axis_index_groups=groups, tiled=True)  131 us
    all_to_all x9, starting transfers between devices, exchange(): lax.all_to_all(blocks, axis, 0, 0, axis_index_groups=groups, tiled=True)  64.7 us
    pallas_call x1, Pallas kernels, backward(): pl.pallas_call(backward_kernel, grid=(STEPS,), in_specs=[pl.BlockSpec(mem...  28.9 us
    all_to_all x1, blocking collectives, exchange(): lax.all_to_all(blocks, axis, 0, 0, axis_index_groups=groups, tiled=True)  16.3 us
    pallas_call x1, Pallas kernels, forward(): pl.pallas_call(forward_kernel, grid=(STEPS,), in_specs=[pl.BlockSpec((SEQ...  13.2 us
    pallas_call x1, Pallas kernels, output(): pl.pallas_call(output_kernel, grid=(POS // ROWS,), in_specs=[pl.BlockSpec...  8.13 us
    unnamed x17, local copies, waits for them, and re-layouts  8 us
    ppermute x1, starting transfers between devices, body(): small = lax.ppermute(small, ('dp', 'seq'), turn)  6.9 us
  transfers between devices with their start and end apart: 13, of which 9 were waited for; matrix products, arithmetic and copies ran while one was open for 9% of the time, Pallas kernels for 16%

profile of v1, /device:TPU:1, one launch (start us, length us, event | category | flops | bytes accessed | tf_op | source)
XLA Modules:
  0.0 306.9 jit_solution(18014797179771080443)
XLA Ops:
  0.6 0.0 copy-start.7
  0.6 0.0 copy-start.2
  0.7 10.2 %all-to-all-start = ((bf16[16,48,1152]{2,1,0:T(8,128)(2,1)}), bf16[16,48,1152]{2,1,0:T(8,128)(2,1)S(1)}, u32[]{:S(2)}, u32[]{:S(2)}) async-start(bf16[16,48,1152]{2,1,0:T(8,128)(2,1)} %bitcast.23), calls=%async_computation | async-start | bytes 3538944 | tf_op jit(solution)/shard_map/all_to_all | solution.py:260
  10.9 0.0 copy-done.7
  10.9 0.7 bitcast_add_fusion.mod_ref
  11.6 0.6 copy-done.6
  12.2 3.6 %fusion.3 = bf16[768,576]{0,1:T(8,128)(2,1)} fusion(bf16[576,1152]{1,0:T(8,128)(2,1)} %w_ref.3, f32[1152]{0:T(1024)S(1)} %slice_reduce_fusion, bf16[1,1,768,1152]{3,2,1,0:T(8,128)(2,1)S(1)} %copy-done.2), kind=kOutput, calls=%fused_computation.7 | convolution fusion | flops 1022312448 | bytes 3985920 | tf_op jit(solution)/shard_map/dot_general | solution.py:34
  15.8 2.2 copy.36
  18.1 33.1 %all-to-all-done.x_ref = bf16[16,48,1152]{2,1,0:T(8,128)(2,1)S(1)} async-done(((bf16[16,48,1152]{2,1,0:T(8,128)(2,1)}), bf16[16,48,1152]{2,1,0:T(8,128)(2,1)S(1)}, u32[]{:S(2)}, u32[]{:S(2)}) %all-to-all-start) | async-done | bytes 1769504 | tf_op jit(solution)/shard_map/all_to_all | solution.py:260
  51.2 6.8 %all-to-all-start.2 = ((bf16[16,48,576]{2,1,0:T(8,128)(2,1)}), bf16[16,48,576]{2,1,0:T(8,128)(2,1)S(1)}, u32[]{:S(2)}, u32[]{:S(2)}) async-start(bf16[16,48,576]{2,1,0:T(8,128)(2,1)} %bitcast.6), calls=%async_computation.2 | async-start | bytes 1966080 | tf_op jit(solution)/shard_map/all_to_all | solution.py:260
  58.0 6.4 %copy.35.w_ref = bf16[1152,1728]{1,0:T(8,128)(2,1)} copy(bf16[1152,1728]{0,1:T(8,128)(2,1)} %param.9) | data formatting | bytes 7962624 | tf_op args[3]
  64.4 0.0 copy-done.1
  64.4 13.2 %forward.1 = (bf16[16,48,1728]{2,1,0:T(8,128)(2,1)}, bf16[16,48,576]{2,1,0:T(8,128)(2,1)}) custom-call(bf16[16,48,1152]{2,1,0:T(8,128)(2,1)} %copy-done.1, f32[3,1152]{1,0:T(4,128)} %copy-done.6, bf16[1152,1728]{1,0:T(8,128)(2,1)} %copy.35.w_ref), custom_call_target="tpu_custom_call" | custom-call | flops 9172942848 | bytes 12000000 | tf_op jit(solution)/shard_map/forward/pallas_call | solution.py:74
  77.6 4.4 %all-to-all-done.2.gm_ref = bf16[16,48,576]{2,1,0:T(8,128)(2,1)S(1)} async-done(((bf16[16,48,576]{2,1,0:T(8,128)(2,1)}), bf16[16,48,576]{2,1,0:T(8,128)(2,1)S(1)}, u32[]{:S(2)}, u32[]{:S(2)}) %all-to-all-start.2) | async-done | bytes 884768 | tf_op jit(solution)/shard_map/all_to_all | solution.py:260
  82.0 6.2 %all-to-all-start.1 = ((bf16[16,48,576]{2,1,0:T(8,128)(2,1)}), bf16[16,48,576]{2,1,0:T(8,128)(2,1)S(1)}, u32[]{:S(2)}, u32[]{:S(2)}) async-start(bf16[16,48,576]{2,1,0:T(8,128)(2,1)} %get-tuple-element.15), calls=%async_computation.1 | async-start | bytes 1966080 | tf_op jit(solution)/shard_map/all_to_all | solution.py:260
  88.2 28.9 %backward.1 = (bf16[16,48,1152]{2,1,0:T(8,128)(2,1)}, bf16[8,72,1728]{2,1,0:T(8,128)(2,1)}, bf16[8,72,1728]{2,1,0:T(8,128)(2,1)}, f32[8,1152]{1,0:T(8,128)}) custom-call(s32[1]{0:T(128)} %bitcast.core_ref, bf16[16,48,1152]{2,1,0:T(8,128)(2,1)} %copy-done.1, bf16[16,48,1728]{2,1,0:T(8,128)(2,1)} %get-tuple-element.17.packed_ref, ...), custom_call_target="tpu_custom_call" | custom-call | flops 15288238080 | bytes 20000000 | tf_op jit(solution)/shard_map/backward/pallas_call | solution.py:158
  117.2 1.6 collective-permute-start
  118.7 0.8 slice.18
  119.5 0.0 all-to-all-done.1
  119.5 0.9 copy-done.4
  120.5 8.1 %output.1 = (bf16[768,1152]{1,0:T(8,128)(2,1)}, bf16[8,36,1152]{2,1,0:T(8,128)(2,1)}, bf16[8,36,1152]{2,1,0:T(8,128)(2,1)}, f32[8,1152]{1,0:T(8,128)}) custom-call(s32[1]{0:T(128)} %bitcast.core_ref, bf16[768,576]{1,0:T(8,128)(2,1)} %bitcast.27, bf16[768,1152]{1,0:T(8,128)(2,1)} %bitcast.24, bf16[768,1152]{1,0:T(8,128)(2,1)} %bitcast.25, ...), custom_call_target="tpu_custom_call" | custom-call | flops 2038431744 | bytes 9000000 | tf_op jit(solution)/shard_map/output/pallas_call | solution.py:227
  128.6 0.0 copy-start.5
  128.6 0.8 slice.19
  129.4 1.2 copy.38
  130.6 0.1 collective-permute-start.1
  130.8 0.8 collective-permute-start.3
  131.6 1.3 collective-permute-done.3
  132.9 0.7 broadcast_in_dim.10
  133.6 6.4 %all-to-all-start.8 = ((f32[8,3,1152]{2,1,0:T(4,128)}), f32[8,3,1152]{2,1,0:T(4,128)}, u32[]{:S(2)}, u32[]{:S(2)}) async-start(f32[8,3,1152]{2,1,0:T(4,128)} %broadcast_in_dim.10), calls=%async_computation.8 | async-start | bytes 294912 | tf_op jit(solution)/shard_map/all_to_all | solution.py:260
  139.9 0.0 collective-permute-done.1
  139.9 1.0 add_convert_fusion.1
  140.9 6.1 %all-to-all-done.8 = f32[8,3,1152]{2,1,0:T(4,128)} async-done(((f32[8,3,1152]{2,1,0:T(4,128)}), f32[8,3,1152]{2,1,0:T(4,128)}, u32[]{:S(2)}, u32[]{:S(2)}) %all-to-all-start.8) | async-done | bytes 110624 | tf_op jit(solution)/shard_map/all_to_all | solution.py:260
  147.0 3.5 %all-to-all-start.5 = ((bf16[8,36,1152]{2,1,0:T(8,128)(2,1)}), bf16[8,36,1152]{2,1,0:T(8,128)(2,1)S(1)}, u32[]{:S(2)}, u32[]{:S(2)}) async-start(bf16[8,36,1152]{2,1,0:T(8,128)(2,1)} %add_convert_fusion.1), calls=%async_computation.5 | async-start | bytes 1474560 | tf_op jit(solution)/shard_map/all_to_all | solution.py:260
  150.6 0.0 collective-permute-done
  150.6 3.4 %add_convert_fusion = bf16[8,72,1728]{2,1,0:T(8,128)(2,1)} fusion(bf16[8,72,1728]{2,1,0:T(8,128)(2,1)} %collective-permute-done, bf16[8,72,1728]{2,1,0:T(8,128)(2,1)S(1)} %copy-done), kind=kLoop, calls=%fused_computation | loop fusion | flops 3981312 | bytes 5971968 | tf_op jit(solution)/shard_map/convert_element_type | solution.py:291
  154.0 6.6 %all-to-all-done.5 = bf16[8,36,1152]{2,1,0:T(8,128)(2,1)S(1)} async-done(((bf16[8,36,1152]{2,1,0:T(8,128)(2,1)}), bf16[8,36,1152]{2,1,0:T(8,128)(2,1)S(1)}, u32[]{:S(2)}, u32[]{:S(2)}) %all-to-all-start.5) | async-done | bytes 663584 | tf_op jit(solution)/shard_map/all_to_all | solution.py:260
  160.6 6.7 %all-to-all-start.4 = ((bf16[8,72,1728]{2,1,0:T(8,128)(2,1)}), bf16[8,72,1728]{2,1,0:T(8,128)(2,1)S(1)}, u32[]{:S(2)}, u32[]{:S(2)}) async-start(bf16[8,72,1728]{2,1,0:T(8,128)(2,1)} %add_convert_fusion), calls=%async_computation.4 | async-start | bytes 4128768 | tf_op jit(solution)/shard_map/all_to_all | solution.py:260
  167.3 0.9 reduce_sum.48
  168.2 24.9 %all-to-all-done.4 = bf16[8,72,1728]{2,1,0:T(8,128)(2,1)S(1)} async-done(((bf16[8,72,1728]{2,1,0:T(8,128)(2,1)}), bf16[8,72,1728]{2,1,0:T(8,128)(2,1)S(1)}, u32[]{:S(2)}, u32[]{:S(2)}) %all-to-all-start.4) | async-done | bytes 1990688 | tf_op jit(solution)/shard_map/all_to_all | solution.py:260
  193.1 0.8 broadcast_in_dim.11
  193.8 7.0 %all-to-all-start.9 = ((f32[16,3,1152]{2,1,0:T(4,128)}), f32[16,3,1152]{2,1,0:T(4,128)S(1)}, u32[]{:S(2)}, u32[]{:S(2)}) async-start(f32[16,3,1152]{2,1,0:T(4,128)} %broadcast_in_dim.11), calls=%async_computation.9 | async-start | bytes 589824 | tf_op jit(solution)/shard_map/all_to_all | solution.py:260
  200.8 0.1 reduce.1
  201.0 0.3 reshape.53
  201.2 0.3 reduce
  201.6 0.6 reshape.52
  202.2 0.1 fusion.6
  202.3 0.1 copy.40
  202.4 8.9 %all-to-all-done.9 = f32[16,3,1152]{2,1,0:T(4,128)S(1)} async-done(((f32[16,3,1152]{2,1,0:T(4,128)}), f32[16,3,1152]{2,1,0:T(4,128)S(1)}, u32[]{:S(2)}, u32[]{:S(2)}) %all-to-all-start.9) | async-done | bytes 221216 | tf_op jit(solution)/shard_map/all_to_all | solution.py:260
  211.3 16.3 %all_to_all.50 = bf16[16,112,128]{2,1,0:T(8,128)(2,1)S(1)} all-to-all(bf16[16,112,128]{2,1,0:T(8,128)(2,1)S(1)} %copy.40), channel_id=1, replica_groups=mesh['dp'=16,'seq'=16] {'seq'}, dimensions={0} | all-to-all | bytes 917504 | tf_op jit(solution)/shard_map/all_to_all | solution.py:260
  227.6 4.3 %all-to-all-start.3 = ((bf16[16,48,1152]{2,1,0:T(8,128)(2,1)}), bf16[16,48,1152]{2,1,0:T(8,128)(2,1)S(1)}, u32[]{:S(2)}, u32[]{:S(2)}) async-start(bf16[16,48,1152]{2,1,0:T(8,128)(2,1)} %get-tuple-element.18), calls=%async_computation.3 | async-start | bytes 3538944 | tf_op jit(solution)/shard_map/all_to_all | solution.py:260
  231.9 0.1 convert_reduce_fusion
  232.0 6.9 %collective-permute-start.2 = (f32[112,128]{1,0:T(8,128)S(1)}, f32[112,128]{1,0:T(8,128)S(1)}, u32[]{:S(2)}, u32[]{:S(2)}) collective-permute-start(f32[112,128]{1,0:T(8,128)S(1)} %broadcast_multiply_fusion), channel_id=1, source_target_pairs={{0,0},{1,16},{2,32},{3,48},{4,64},{5,80},{6,96},{7,112},{8,128},{9... | collective-permute-start | bytes 172040 | tf_op jit(solution)/shard_map/ppermute | solution.py:311
  238.9 0.1 reduce_sum.49
  239.0 35.3 %all-to-all-done.3 = bf16[16,48,1152]{2,1,0:T(8,128)(2,1)S(1)} async-done(((bf16[16,48,1152]{2,1,0:T(8,128)(2,1)}), bf16[16,48,1152]{2,1,0:T(8,128)(2,1)S(1)}, u32[]{:S(2)}, u32[]{:S(2)}) %all-to-all-start.3) | async-done | bytes 1769504 | tf_op jit(solution)/shard_map/all_to_all | solution.py:260
  274.3 0.0 collective-permute-done.2
  274.3 1.0 broadcast_in_dim.9
  275.3 13.6 %all-to-all-start.7 = ((f32[16,112,128]{2,1,0:T(8,128)}), f32[16,112,128]{2,1,0:T(8,128)S(1)}, u32[]{:S(2)}, u32[]{:S(2)}) async-start(f32[16,112,128]{2,1,0:T(8,128)} %broadcast_in_dim.9), calls=%async_computation.7 | async-start | bytes 1835008 | tf_op jit(solution)/shard_map/all_to_all | solution.py:260
  288.9 0.6 broadcast_multiply_fusion.1
  289.5 3.1 %fusion = bf16[1,1,768,1152]{3,2,1,0:T(8,128)(2,1)} fusion(bf16[1,1,768,1152]{3,2,1,0:T(8,128)(2,1)S(1)} %bitcast.22, bf16[1,1,768,1152]{3,2,1,0:T(8,128)(2,1)} %param.11), kind=kLoop, calls=%fused_computation.2 | loop fusion | flops 3538944 | bytes 5308416 | tf_op jit(solution)/shard_map/convert_element_type | solution.py:282
  292.6 12.1 %all-to-all-done.7 = f32[16,112,128]{2,1,0:T(8,128)S(1)} async-done(((f32[16,112,128]{2,1,0:T(8,128)}), f32[16,112,128]{2,1,0:T(8,128)S(1)}, u32[]{:S(2)}, u32[]{:S(2)}) %all-to-all-start.7) | async-done | bytes 917536 | tf_op jit(solution)/shard_map/all_to_all | solution.py:260
  304.8 0.1 copy.42
  304.8 0.9 reshape.55
  305.7 0.1 copy.41
  305.8 1.1 reshape.54
  (15 shorter events, 0.1 us)
Async XLA Ops:
  0.6 10.2 %copy-start.7 = (f32[1,3,1152]{2,0,1:T(1,128)S(1)}, f32[1,3,1152]{2,0,1:T(1,128)}, u32[]{:S(2)}) copy-start(f32[1,3,1152]{2,0,1:T(1,128)} %param.7) | copy-start | bytes 41476
  0.6 11.6 %copy-start.2 = (bf16[1,1,768,1152]{3,2,1,0:T(8,128)(2,1)S(1)}, bf16[1,1,768,1152]{3,2,1,0:T(8,128)(2,1)}, u32[]{:S(2)}) copy-start(bf16[1,1,768,1152]{3,2,1,0:T(8,128)(2,1)} %param.11) | copy-start | bytes 5308420
  0.7 50.6 %all-to-all-start = ((bf16[16,48,1152]{2,1,0:T(8,128)(2,1)}), bf16[16,48,1152]{2,1,0:T(8,128)(2,1)S(1)}, u32[]{:S(2)}, u32[]{:S(2)}) async-start(bf16[16,48,1152]{2,1,0:T(8,128)(2,1)} %bitcast.23), calls=%async_computation | async-start | bytes 3538944 | tf_op jit(solution)/shard_map/all_to_all | solution.py:260
  11.6 0.6 copy-start.6
  51.2 13.2 %copy-start.1 = (bf16[16,48,1152]{2,1,0:T(8,128)(2,1)}, bf16[16,48,1152]{2,1,0:T(8,128)(2,1)S(1)}, u32[]{:S(2)}) copy-start(bf16[16,48,1152]{2,1,0:T(8,128)(2,1)S(1)} %all-to-all-done.x_ref) | copy-start | bytes 5308420
  51.2 30.8 %all-to-all-start.2 = ((bf16[16,48,576]{2,1,0:T(8,128)(2,1)}), bf16[16,48,576]{2,1,0:T(8,128)(2,1)S(1)}, u32[]{:S(2)}, u32[]{:S(2)}) async-start(bf16[16,48,576]{2,1,0:T(8,128)(2,1)} %bitcast.6), calls=%async_computation.2 | async-start | bytes 1966080 | tf_op jit(solution)/shard_map/all_to_all | solution.py:260
  82.0 6.2 %copy-start.3 = (bf16[16,48,576]{2,1,0:T(8,128)(2,1)}, bf16[16,48,576]{2,1,0:T(8,128)(2,1)S(1)}, u32[]{:S(2)}) copy-start(bf16[16,48,576]{2,1,0:T(8,128)(2,1)S(1)} %all-to-all-done.2.gm_ref) | copy-start | bytes 2654212
  82.0 37.5 %all-to-all-start.1 = ((bf16[16,48,576]{2,1,0:T(8,128)(2,1)}), bf16[16,48,576]{2,1,0:T(8,128)(2,1)S(1)}, u32[]{:S(2)}, u32[]{:S(2)}) async-start(bf16[16,48,576]{2,1,0:T(8,128)(2,1)} %get-tuple-element.15), calls=%async_computation.1 | async-start | bytes 1966080 | tf_op jit(solution)/shard_map/all_to_all | solution.py:260
  117.2 33.4 %collective-permute-start = (bf16[8,72,1728]{2,1,0:T(8,128)(2,1)}, bf16[8,72,1728]{2,1,0:T(8,128)(2,1)}, u32[]{:S(2)}, u32[]{:S(2)}) collective-permute-start(bf16[8,72,1728]{2,1,0:T(8,128)(2,1)} %get-tuple-element.20), channel_id=1, source_target_pairs={{0,16},{16,0},{32,48},{48,32},{64,80},{80,64},{96,112},{112,96},{1... | collective-permute-start | bytes 5971976 | tf_op jit(solution)/shard_map/ppermute | solution.py:290
  119.5 0.9 copy-start.4
  128.6 11.3 %copy-start.5 = (bf16[8,36,1152]{2,1,0:T(8,128)(2,1)S(1)}, bf16[8,36,1152]{2,1,0:T(8,128)(2,1)}, u32[]{:S(2)}) copy-start(bf16[8,36,1152]{2,1,0:T(8,128)(2,1)} %get-tuple-element.21) | copy-start | bytes 1990660
  130.6 9.3 %collective-permute-start.1 = (bf16[8,36,1152]{2,0,1:T(8,128)(2,1)S(1)}, bf16[8,36,1152]{2,0,1:T(8,128)(2,1)S(1)}, u32[]{:S(2)}, u32[]{:S(2)}) collective-permute-start(bf16[8,36,1152]{2,0,1:T(8,128)(2,1)S(1)} %copy.38), channel_id=1, source_target_pairs={{0,16},{16,0},{32,48},{48,32},{64,80},{80,64},{96,112},{112,96},{1... | collective-permute-start | bytes 1990664 | tf_op jit(solution)/shard_map/ppermute | solution.py:290
  130.8 2.1 collective-permute-start.3
  133.6 13.5 %all-to-all-start.8 = ((f32[8,3,1152]{2,1,0:T(4,128)}), f32[8,3,1152]{2,1,0:T(4,128)}, u32[]{:S(2)}, u32[]{:S(2)}) async-start(f32[8,3,1152]{2,1,0:T(4,128)} %broadcast_in_dim.10), calls=%async_computation.8 | async-start | bytes 294912 | tf_op jit(solution)/shard_map/all_to_all | solution.py:260
  139.9 10.7 %copy-start = (bf16[8,72,1728]{2,1,0:T(8,128)(2,1)S(1)}, bf16[8,72,1728]{2,1,0:T(8,128)(2,1)}, u32[]{:S(2)}) copy-start(bf16[8,72,1728]{2,1,0:T(8,128)(2,1)} %get-tuple-element.19) | copy-start | bytes 5971972
  147.0 13.5 %all-to-all-start.5 = ((bf16[8,36,1152]{2,1,0:T(8,128)(2,1)}), bf16[8,36,1152]{2,1,0:T(8,128)(2,1)S(1)}, u32[]{:S(2)}, u32[]{:S(2)}) async-start(bf16[8,36,1152]{2,1,0:T(8,128)(2,1)} %add_convert_fusion.1), calls=%async_computation.5 | async-start | bytes 1474560 | tf_op jit(solution)/shard_map/all_to_all | solution.py:260
  160.6 32.5 %all-to-all-start.4 = ((bf16[8,72,1728]{2,1,0:T(8,128)(2,1)}), bf16[8,72,1728]{2,1,0:T(8,128)(2,1)S(1)}, u32[]{:S(2)}, u32[]{:S(2)}) async-start(bf16[8,72,1728]{2,1,0:T(8,128)(2,1)} %add_convert_fusion), calls=%async_computation.4 | async-start | bytes 4128768 | tf_op jit(solution)/shard_map/all_to_all | solution.py:260
  193.8 17.4 %all-to-all-start.9 = ((f32[16,3,1152]{2,1,0:T(4,128)}), f32[16,3,1152]{2,1,0:T(4,128)S(1)}, u32[]{:S(2)}, u32[]{:S(2)}) async-start(f32[16,3,1152]{2,1,0:T(4,128)} %broadcast_in_dim.11), calls=%async_computation.9 | async-start | bytes 589824 | tf_op jit(solution)/shard_map/all_to_all | solution.py:260
  227.6 46.7 %all-to-all-start.3 = ((bf16[16,48,1152]{2,1,0:T(8,128)(2,1)}), bf16[16,48,1152]{2,1,0:T(8,128)(2,1)S(1)}, u32[]{:S(2)}, u32[]{:S(2)}) async-start(bf16[16,48,1152]{2,1,0:T(8,128)(2,1)} %get-tuple-element.18), calls=%async_computation.3 | async-start | bytes 3538944 | tf_op jit(solution)/shard_map/all_to_all | solution.py:260
  232.0 42.3 %collective-permute-start.2 = (f32[112,128]{1,0:T(8,128)S(1)}, f32[112,128]{1,0:T(8,128)S(1)}, u32[]{:S(2)}, u32[]{:S(2)}) collective-permute-start(f32[112,128]{1,0:T(8,128)S(1)} %broadcast_multiply_fusion), channel_id=1, source_target_pairs={{0,0},{1,16},{2,32},{3,48},{4,64},{5,80},{6,96},{7,112},{8,128},{9... | collective-permute-start | bytes 172040 | tf_op jit(solution)/shard_map/ppermute | solution.py:311
  275.3 29.4 %all-to-all-start.7 = ((f32[16,112,128]{2,1,0:T(8,128)}), f32[16,112,128]{2,1,0:T(8,128)S(1)}, u32[]{:S(2)}, u32[]{:S(2)}) async-start(f32[16,112,128]{2,1,0:T(8,128)} %broadcast_in_dim.9), calls=%async_computation.7 | async-start | bytes 1835008 | tf_op jit(solution)/shard_map/all_to_all | solution.py:260

commit v2 on v1

v2 whole, which is shorter than its diff:
```python
import functools
import math

import jax
import jax.numpy as jnp
from jax import lax
from jax.experimental import pallas as pl
from jax.experimental.pallas import tpu as pltpu
from jax.sharding import PartitionSpec as P

D = 1152
HEAD_DIM = 72
HEADS = 8
POS = 768
INNER = 576
SEQ = 16
DP = 16
CHIPS = DP // 2
HERE = POS // SEQ
TILE = 16
HALF = 8
ROWS = SEQ * TILE
UNIT = SEQ * HALF
PAIR = 2 * HEAD_DIM
QKV_ROWS = 64
OUT_ROWS = 24
BLOCK_ROWS = QKV_ROWS + OUT_ROWS
STEPS = HERE // TILE
EPSILON = 1e-06
SCALE = 1.0 / math.sqrt(HEAD_DIM)
BF = jnp.bfloat16
F32 = jnp.float32
PARAMS = pltpu.CompilerParams(
    dimension_semantics=("arbitrary",), vmem_limit_bytes=56 * 1024 * 1024
)
WHOLE = pltpu.CompilerParams(vmem_limit_bytes=40 * 1024 * 1024)
NT = (((1,), (1,)), ((), ()))
TN = (((0,), (0,)), ((), ()))


def dot(a, b, dims=(((1,), (0,)), ((), ()))):
    return lax.dot_general(a, b, dims, preferred_element_type=F32)


def normalize(x):
    centered = x - jnp.mean(x, axis=1, keepdims=True)
    inv_std = lax.rsqrt(jnp.mean(centered * centered, axis=1, keepdims=True) + EPSILON)
    return centered * inv_std, inv_std


def load_rows(block):
    wide = block.astype(F32)
    width = wide.shape[-1]
    return jnp.concatenate(
        [wide[:, :HALF].reshape(UNIT, width), wide[:, HALF:].reshape(UNIT, width)], axis=0
    )


def store_rows(rows):
    width = rows.shape[-1]
    halves = [rows[h * UNIT : h * UNIT + UNIT].reshape(SEQ, HALF, width) for h in range(2)]
    return jnp.concatenate(halves, axis=1).astype(BF)


def position_mask():
    rows = lax.broadcasted_iota(jnp.int32, (HALF, UNIT), 0)
    cols = lax.broadcasted_iota(jnp.int32, (HALF, UNIT), 1) % HALF
    return jnp.where(rows == cols, 1.0, 0.0).astype(F32)


def first_lanes(dtype):
    lanes = lax.broadcasted_iota(jnp.int32, (1, PAIR), 1)
    return jnp.where(lanes < HEAD_DIM, 1.0, 0.0).astype(dtype)


def spread(pair, first):
    return jnp.concatenate([pair * first, pair * (1 - first)], axis=0)


def gather(rows, first):
    return rows[:UNIT] * first + rows[UNIT:] * (1 - first)


def by_frame(rows):
    return rows.reshape(2, SEQ, HALF, UNIT)


def softmax(queries, keys_spread, mask):
    scores = by_frame(dot(keys_spread, queries, NT) * SCALE)
    exp_scores = jnp.exp(scores - jnp.max(scores, axis=1, keepdims=True))
    return exp_scores * (mask / jnp.sum(exp_scores, axis=1, keepdims=True))


def flat(weights):
    return weights.reshape(2 * UNIT, UNIT).astype(BF)


def pair_of(rows, part, n):
    start = part * INNER + n * PAIR
    return rows[:, start : start + PAIR]


def forward_kernel(x_ref, mod_ref, w_ref, packed_ref, mixed_ref):
    normed, _ = normalize(load_rows(x_ref[...]))
    modulated = (normed * (1.0 + mod_ref[1:2, :]) + mod_ref[0:1, :]).astype(BF)
    packed = dot(modulated, w_ref[...], NT).astype(BF)
    packed_ref[...] = packed
    mask, first = position_mask(), first_lanes(BF)
    units = []
    for u in range(2):
        rows = packed[u * UNIT : u * UNIT + UNIT]
        pieces = []
        for n in range(HEADS // 2):
            weights = softmax(pair_of(rows, 0, n), spread(pair_of(rows, 1, n), first), mask)
            pieces.append(dot(flat(weights), spread(pair_of(rows, 2, n), first), TN))
        units.append(jnp.concatenate(pieces, axis=1))
    mixed_ref[...] = store_rows(jnp.concatenate(units, axis=0))


def forward(x, modulation, w_turned):
    return pl.pallas_call(
        forward_kernel,
        grid=(STEPS,),
        in_specs=[
            pl.BlockSpec((SEQ, TILE, D), lambda j: (0, j, 0)),
            pl.BlockSpec((3, D), lambda j: (0, 0)),
            pl.BlockSpec((3 * INNER, D), lambda j: (0, 0)),
        ],
        out_specs=[
            pl.BlockSpec((ROWS, 3 * INNER), lambda j: (j, 0)),
            pl.BlockSpec((SEQ, TILE, INNER), lambda j: (0, j, 0)),
        ],
        out_shape=[
            jax.ShapeDtypeStruct((POS, 3 * INNER), BF),
            jax.ShapeDtypeStruct((SEQ, HERE, INNER), BF),
        ],
        compiler_params=PARAMS,
        cost_estimate=pl.CostEstimate(
            flops=2 * POS * D * 3 * INNER * 2, bytes_accessed=12_000_000, transcendentals=800_000
        ),
        name="forward",
    )(x, modulation, w_turned)


def grad_mixed_kernel(grad_ref, mod_ref, w_ref, out_ref):
    grad_branch = (grad_ref[...].astype(F32) * mod_ref[2:3, :]).astype(BF)
    out_ref[...] = dot(grad_branch, w_ref[...], NT).astype(BF)


def grad_mixed_rows(out_grad, modulation, w_out):
    return pl.pallas_call(
        grad_mixed_kernel,
        grid=(POS // ROWS,),
        in_specs=[
            pl.BlockSpec((ROWS, D), lambda j: (j, 0)),
            pl.BlockSpec((3, D), lambda j: (0, 0)),
            pl.BlockSpec((INNER, D), lambda j: (0, 0)),
        ],
        out_specs=pl.BlockSpec((ROWS, INNER), lambda j: (j, 0)),
        out_shape=jax.ShapeDtypeStruct((POS, INNER), BF),
        compiler_params=PARAMS,
        cost_estimate=pl.CostEstimate(
            flops=2 * POS * D * INNER, bytes_accessed=4_000_000, transcendentals=0
        ),
        name="grad_mixed",
    )(out_grad, modulation, w_out)


def backward_kernel(
    place_ref, x_ref, gm_ref, packed_ref, mod_ref, w_ref,
    delta_ref, keep_ref, send_ref, table_ref,
    modulated_all, gp_all, total,
):
    step = pl.program_id(0)
    normed, inv_std = normalize(load_rows(x_ref[...]))
    scale_row = 1.0 + mod_ref[1:2, :]
    here = pl.ds(pl.multiple_of(step * ROWS, ROWS), ROWS)
    modulated_all[here, :] = (normed * scale_row + mod_ref[0:1, :]).astype(BF)
    grad_mixed = load_rows(gm_ref[...]).astype(BF)
    packed = packed_ref[...]
    mask, first, first_wide = position_mask(), first_lanes(BF), first_lanes(F32)
    units = []
    for u in range(2):
        rows = packed[u * UNIT : u * UNIT + UNIT]
        grad_rows = grad_mixed[u * UNIT : u * UNIT + UNIT]
        pieces = [[], [], []]
        for n in range(HEADS // 2):
            queries = pair_of(rows, 0, n)
            keys_spread = spread(pair_of(rows, 1, n), first)
            values_spread = spread(pair_of(rows, 2, n), first)
            grad_pair = pair_of(grad_rows, 0, n)
            weights = softmax(queries, keys_spread, mask)
            grad_weights = by_frame(dot(values_spread, grad_pair, NT))
            row_total = jnp.sum(weights * grad_weights, axis=1, keepdims=True)
            grad_scores = flat(weights * (grad_weights - row_total) * SCALE)
            pieces[0].append(dot(grad_scores, keys_spread, TN).astype(BF))
            pieces[1].append(gather(dot(grad_scores, queries), first_wide).astype(BF))
            pieces[2].append(gather(dot(flat(weights), grad_pair), first_wide).astype(BF))
        units.append(jnp.concatenate(pieces[0] + pieces[1] + pieces[2], axis=1))
    grad_packed = jnp.concatenate(units, axis=0)
    gp_all[here, :] = grad_packed
    grad_mod = dot(grad_packed, w_ref[...])
    shift_sum = jnp.sum(grad_mod, axis=0, keepdims=True)
    scale_sum = jnp.sum(grad_mod * normed, axis=0, keepdims=True)
    grad_normed = grad_mod * scale_row
    delta = inv_std * (
        grad_normed
        - jnp.mean(grad_normed, axis=1, keepdims=True)
        - normed * jnp.mean(grad_normed * normed, axis=1, keepdims=True)
    )
    delta_ref[...] = store_rows(delta)

    @pl.when(step == 0)
    def _():
        table_ref[...] = jnp.zeros_like(table_ref)

    table_ref[0:1, :] += shift_sum
    table_ref[1:2, :] += scale_sum

    @pl.when(step == STEPS - 1)
    def _():
        for r in range(3):
            part = slice(r * 384, r * 384 + 384)
            total[part, :] = dot(modulated_all[:, part], gp_all[...], TN)
        core = place_ref[0]
        rows = D // DP
        for k in range(CHIPS):
            chip = k % 2 * 4 + k // 2
            mine = pl.multiple_of((2 * chip + core) * rows, 8)
            other = pl.multiple_of((2 * chip + 1 - core) * rows, 8)
            keep_ref[k] = total[pl.ds(mine, rows), :].astype(BF)
            send_ref[k] = total[pl.ds(other, rows), :].astype(BF)


def backward(place, x, grad_mixed, packed, modulation, w_turned):
    half = jax.ShapeDtypeStruct((CHIPS, D // DP, 3 * INNER), BF)
    return pl.pallas_call(
        backward_kernel,
        grid=(STEPS,),
        in_specs=[
            pl.BlockSpec(memory_space=pltpu.SMEM),
            pl.BlockSpec((SEQ, TILE, D), lambda j: (0, j, 0)),
            pl.BlockSpec((SEQ, TILE, INNER), lambda j: (0, j, 0)),
            pl.BlockSpec((ROWS, 3 * INNER), lambda j: (j, 0)),
            pl.BlockSpec((3, D), lambda j: (0, 0)),
            pl.BlockSpec((3 * INNER, D), lambda j: (0, 0)),
        ],
        out_specs=[
            pl.BlockSpec((SEQ, TILE, D), lambda j: (0, j, 0)),
            pl.BlockSpec(half.shape, lambda j: (0, 0, 0)),
            pl.BlockSpec(half.shape, lambda j: (0, 0, 0)),
            pl.BlockSpec((8, D), lambda j: (0, 0)),
        ],
        out_shape=[
            jax.ShapeDtypeStruct((SEQ, HERE, D), BF),
            half,
            half,
            jax.ShapeDtypeStruct((8, D), F32),
        ],
        scratch_shapes=[
            pltpu.VMEM((POS, D), BF),
            pltpu.VMEM((POS, 3 * INNER), BF),
            pltpu.VMEM((D, 3 * INNER), F32),
        ],
        compiler_params=PARAMS,
        cost_estimate=pl.CostEstimate(
            flops=2 * POS * D * 3 * INNER * 4, bytes_accessed=20_000_000, transcendentals=800_000
        ),
        name="backward",
    )(place, x, grad_mixed, packed, modulation, w_turned)


def output_kernel(
    place_ref, mixed_ref, x_ref, grad_ref, mod_ref, w_ref, table_ref,
    out_ref, keep_ref, send_ref, total, gate_total,
):
    step = pl.program_id(0)
    gate_row = mod_ref[2:3, :]
    mixed = mixed_ref[...]
    branch = dot(mixed, w_ref[...])
    out_ref[...] = (x_ref[...].astype(F32) + gate_row * branch).astype(BF)
    grad_out = grad_ref[...].astype(F32)
    gate_sum = jnp.sum(grad_out * branch, axis=0, keepdims=True)
    term = dot(mixed, (grad_out * gate_row).astype(BF), TN)

    @pl.when(step == 0)
    def _():
        total[...] = jnp.zeros_like(total)
        gate_total[...] = jnp.zeros_like(gate_total)

    total[...] += term
    gate_total[0:1, :] += gate_sum

    @pl.when(step == POS // ROWS - 1)
    def _():
        rows = INNER // DP
        core = place_ref[0]
        table = jnp.concatenate(
            [table_ref[0:2, :], gate_total[0:1, :], jnp.zeros((1, D), F32)], axis=0
        )
        for k in range(CHIPS):
            chip = k % 2 * 4 + k // 2
            both = total[2 * chip * rows : 2 * (chip + 1) * rows, :]
            first = jnp.concatenate([both[:rows], table], axis=0).astype(BF)
            second = jnp.concatenate([both[rows:], table], axis=0).astype(BF)
            keep_ref[k] = jnp.where(core == 0, first, second)
            send_ref[k] = jnp.where(core == 0, second, first)


def output(place, mixed, x, out_grad, modulation, w_out, table):
    half = jax.ShapeDtypeStruct((CHIPS, INNER // DP + 4, D), BF)
    return pl.pallas_call(
        output_kernel,
        grid=(POS // ROWS,),
        in_specs=[
            pl.BlockSpec(memory_space=pltpu.SMEM),
            pl.BlockSpec((ROWS, INNER), lambda j: (j, 0)),
            pl.BlockSpec((ROWS, D), lambda j: (j, 0)),
            pl.BlockSpec((ROWS, D), lambda j: (j, 0)),
            pl.BlockSpec((3, D), lambda j: (0, 0)),
            pl.BlockSpec((INNER, D), lambda j: (0, 0)),
            pl.BlockSpec((8, D), lambda j: (0, 0)),
        ],
        out_specs=[
            pl.BlockSpec((ROWS, D), lambda j: (j, 0)),
            pl.BlockSpec(half.shape, lambda j: (0, 0, 0)),
            pl.BlockSpec(half.shape, lambda j: (0, 0, 0)),
        ],
        out_shape=[jax.ShapeDtypeStruct((POS, D), BF), half, half],
        scratch_shapes=[pltpu.VMEM((INNER, D), F32), pltpu.VMEM((8, D), F32)],
        compiler_params=PARAMS,
        cost_estimate=pl.CostEstimate(
            flops=4 * POS * D * INNER, bytes_accessed=9_000_000, transcendentals=0
        ),
        name="output",
    )(place, mixed, x, out_grad, modulation, w_out, table)


def whole_call(kernel, name, out_shape, *args, scratch=(), smem=0):
    out_specs = jax.tree.map(lambda _: pl.BlockSpec(memory_space=pltpu.VMEM), out_shape)
    return pl.pallas_call(
        kernel,
        in_specs=[pl.BlockSpec(memory_space=pltpu.SMEM)] * smem
        + [pl.BlockSpec(memory_space=pltpu.VMEM)] * (len(args) - smem),
        out_specs=out_specs,
        out_shape=out_shape,
        scratch_shapes=scratch,
        compiler_params=WHOLE,
        cost_estimate=pl.CostEstimate(
            flops=1_000_000, bytes_accessed=sum(2 * a.size for a in args), transcendentals=0
        ),
        name=name,
    )(*args)


def pair_kernel(keep_ref, got_ref, out_ref):
    out_ref[...] = (keep_ref[...].astype(F32) + got_ref[...].astype(F32)).astype(BF)


def pair_sum(keep, got):
    return whole_call(pair_kernel, "pair_sum", jax.ShapeDtypeStruct(keep.shape, BF), keep, got)


def pair_turn_kernel(place_ref, keep_ref, got_ref, *refs):
    total = refs[4]
    total[...] = (keep_ref[...].astype(F32) + got_ref[...].astype(F32)).astype(BF)
    for r in range(4):
        y = lax.rem(place_ref[1] + r, 4)
        for x in range(2):
            refs[r][x] = total[2 * y + x]


def pair_turn(place, keep, got):
    return whole_call(
        pair_turn_kernel,
        "pair_turn",
        [jax.ShapeDtypeStruct((2,) + keep.shape[1:], BF)] * 4,
        place,
        keep,
        got,
        scratch=[pltpu.VMEM(keep.shape, BF)],
        smem=1,
    )


def stacked(block, rows):
    height, width = block.shape
    tiles = [block[:, c : c + 128] for c in range(0, width // 128 * 128, 128)]
    if width % 128:
        last = block[:, width // 128 * 128 :]
        tiles.append(jnp.concatenate([last, jnp.zeros((height, 128 - width % 128), F32)], axis=1))
    tiles.append(jnp.zeros((rows - height * len(tiles), 128), F32))
    return jnp.concatenate(tiles, axis=0)


def unstacked(rows, height, width):
    tiles = [rows[height * c : height * c + height] for c in range(-(-width // 128))]
    return jnp.concatenate(tiles, axis=1)[:, :width]


def pieces_kernel(qkv_ref, o0, o1, o2, o3, pieces_ref):
    parts = []
    for x in range(2):
        out = sum(o[x].astype(F32) for o in (o0, o1, o2, o3))
        parts.append(stacked(qkv_ref[x].astype(F32), SEQ * QKV_ROWS))
        parts.append(stacked(out[: INNER // DP], SEQ * OUT_ROWS))
    table = stacked(jnp.concatenate([out[INNER // DP :], jnp.zeros((4, D), F32)], axis=0)[:3], 32)
    for s in range(SEQ):
        rows = [p[h * s : h * s + h] for p, h in zip(parts, (QKV_ROWS, OUT_ROWS) * 2)]
        pieces_ref[s] = jnp.concatenate(rows + [table], axis=0).astype(BF)


def block_pieces(qkv_blocks, out_blocks):
    return whole_call(
        pieces_kernel,
        "block_pieces",
        jax.ShapeDtypeStruct((SEQ, 2 * BLOCK_ROWS + 32, 128), BF),
        qkv_blocks,
        *out_blocks,
    )


def seq_sum_kernel(factor, place_ref, pieces_ref, own_ref, other_ref):
    total = sum(pieces_ref[k].astype(F32) for k in range(SEQ)) * factor
    first, second = total[:BLOCK_ROWS], total[BLOCK_ROWS : 2 * BLOCK_ROWS]
    table = total[2 * BLOCK_ROWS :]
    own = jnp.where(place_ref[2] == 0, first, second)
    other = jnp.where(place_ref[2] == 0, second, first)
    own_ref[...] = jnp.concatenate([own, table], axis=0)
    other_ref[...] = jnp.concatenate([other, table], axis=0)


def seq_sum(place, pieces, factor):
    return whole_call(
        functools.partial(seq_sum_kernel, factor),
        "seq_sum",
        [jax.ShapeDtypeStruct((BLOCK_ROWS + 32, 128), F32)] * 2,
        place,
        pieces,
        smem=1,
    )


def last_sum_kernel(own_ref, other_ref, pieces_ref, table_ref):
    total = own_ref[...] + other_ref[...]
    piece = total[:BLOCK_ROWS].astype(BF)
    for k in range(DP):
        pieces_ref[k] = piece
    for r in range(3):
        rows = [total[BLOCK_ROWS + 3 * c + r : BLOCK_ROWS + 3 * c + r + 1] for c in range(9)]
        table_ref[r : r + 1, :] = jnp.concatenate(rows, axis=1)


def last_sum(own, other):
    return whole_call(
        last_sum_kernel,
        "last_sum",
        [
            jax.ShapeDtypeStruct((DP, BLOCK_ROWS, 128), BF),
            jax.ShapeDtypeStruct((3, D), F32),
        ],
        own,
        other,
    )


def assemble_kernel(pieces_ref, qkv_ref, out_ref):
    pieces = [pieces_ref[s].astype(F32) for s in range(DP)]
    qkv = jnp.concatenate([p[:QKV_ROWS] for p in pieces], axis=0)
    out = jnp.concatenate([p[QKV_ROWS:] for p in pieces], axis=0)
    qkv_ref[...] = unstacked(qkv, D // SEQ, 3 * INNER)
    out_ref[...] = unstacked(out, INNER // SEQ, D)


def assemble(pieces):
    return whole_call(
        assemble_kernel,
        "assemble",
        [
            jax.ShapeDtypeStruct((D // SEQ, 3 * INNER), F32),
            jax.ShapeDtypeStruct((INNER // SEQ, D), F32),
        ],
        pieces,
    )


def exchange(blocks, axis, groups=None):
    return lax.all_to_all(blocks, axis, 0, 0, axis_index_groups=groups, tiled=True)


def body(clip_tokens, time_mod, mod_table, w_qkv, w_out, out_grad):
    tokens, grad_rows = clip_tokens[0, 0], out_grad[0, 0]
    modulation = mod_table + time_mod[0]
    dp_at = lax.axis_index("dp")
    place = jnp.stack([dp_at % 2, dp_at // 2 % 4, dp_at // 8]).astype(jnp.int32)
    w_turned = w_qkv.T
    x_pos = exchange(tokens.reshape(SEQ, HERE, D), "seq")
    grad_mixed = grad_mixed_rows(grad_rows, modulation, w_out)
    gm_pos = exchange(grad_mixed.reshape(SEQ, HERE, INNER), "seq")
    packed, mixed_pos = forward(x_pos, modulation, w_turned)
    mixed = exchange(mixed_pos, "seq").reshape(POS, INNER)
    delta_pos, qkv_keep, qkv_send, table = backward(
        place, x_pos, gm_pos, packed, modulation, w_turned
    )
    swap = [(i, i ^ 1) for i in range(DP)]
    column = [[8 * x + 2 * y + c for y in range(4)] for x in range(2) for c in range(2)]
    qkv_keep, qkv_send, mixed = lax.optimization_barrier((qkv_keep, qkv_send, mixed))
    qkv_blocks = pair_sum(qkv_keep, lax.ppermute(qkv_send, "dp", swap))
    table = lax.optimization_barrier((table, qkv_blocks))[0]
    qkv_blocks = lax.psum_scatter(
        qkv_blocks, "dp", scatter_dimension=0, axis_index_groups=column, tiled=True
    )
    out_tokens, out_keep, out_send = output(
        place, mixed, tokens, grad_rows, modulation, w_out, table
    )
    out_blocks = list(pair_turn(place, out_keep, lax.ppermute(out_send, "dp", swap)))
    for r in range(1, 4):
        route = [(i, i // 8 * 8 + (i + 2 * r) % 8) for i in range(DP)]
        out_blocks[r] = lax.ppermute(out_blocks[r], "dp", route)
    delta = exchange(delta_pos, "seq")
    pieces, delta = lax.optimization_barrier((block_pieces(qkv_blocks, out_blocks), delta))
    pieces = exchange(pieces, "seq")
    own, other = seq_sum(place, pieces, 1.0 / math.sqrt(DP * SEQ * POS))
    turn = [(i * SEQ + s, s * SEQ + i) for i in range(DP) for s in range(SEQ)]
    turn_other = [(i * SEQ + s, s * SEQ + (i ^ 8)) for i in range(DP) for s in range(SEQ)]
    own = lax.ppermute(own, ("dp", "seq"), turn)
    other = lax.ppermute(other, ("dp", "seq"), turn_other)
    pieces, table = last_sum(own, other)
    qkv_grad, out_weight_grad = assemble(exchange(pieces, "dp"))
    grad_tokens = (grad_rows.astype(F32) + delta.reshape(POS, D).astype(F32)).astype(BF)
    return (
        out_tokens[None, None],
        grad_tokens[None, None],
        qkv_grad,
        out_weight_grad,
        table,
    )


def solution(mesh):
    return jax.shard_map(
        body,
        mesh=mesh,
        in_specs=(
            P("dp", "seq", None, None),
            P("dp", None, None),
            P(),
            P(),
            P(),
            P("dp", "seq", None, None),
        ),
        out_specs=(
            P("dp", "seq", None, None),
            P("dp", "seq", None, None),
            P("seq", None),
            P("seq", None),
            P(),
        ),
        check_vma=False,
    )
```

time: 308 us -> 250 us (0.81)
  waiting for transfers between devices: 133 us -> 78.5 us
  local copies, waits for them, and re-layouts: 18.6 us -> 3.78 us
  between operations: 0.89 us -> 14.2 us
  starting transfers between devices: 74.1 us -> 61 us
  blocking collectives: 16.3 us -> 29.3 us
  Pallas kernels: 50.2 us -> 57.5 us
  other arithmetic: 10.4 us -> 4.43 us
  matrix products: 3.6 us -> 0 us
    all_to_all x9 -> x5, waiting for transfers between devices: 131 us -> 56.8 us  [exchange(): lax.all_to_all(blocks, axis, 0, 0, axis_index_groups=groups, tiled=True)]
    all_to_all x9 -> x5, starting transfers between devices: 64.7 us -> 42.3 us  [exchange(): lax.all_to_all(blocks, axis, 0, 0, axis_index_groups=groups, tiled=True)]
    ppermute x4 -> x7, waiting for transfers between devices: 1.31 us -> 21.7 us  [the longest x3 14.4 us: body(): out_blocks[r] = lax.ppermute(out_blocks[r], 'dp', route)]
    all_to_all x1, blocking collectives: 16.3 us -> 29.3 us  [exchange(): lax.all_to_all(blocks, axis, 0, 0, axis_index_groups=groups, tiled=True)]
    pallas_call x0 -> x7, Pallas kernels: none -> 10.1 us  [the longest x6 5.23 us: whole_call(): pl.pallas_call(kernel, in_specs=[pl.BlockSpec(memory_space=pltpu.SMEM)] *...]
    ppermute x4 -> x7, starting transfers between devices: 9.39 us -> 18.7 us  [the longest x3 5.28 us: body(): out_blocks[r] = lax.ppermute(out_blocks[r], 'dp', route)]
    pallas_call x1, Pallas kernels: 28.9 us -> 23.5 us  [backward(): pl.pallas_call(backward_kernel, grid=(STEPS,), in_specs=[pl.BlockSpec(mem...]
    convert_element_type x3 -> x1, other arithmetic: 7.46 us -> 3.14 us  [body(): (grad_rows.astype(F32) + delta.reshape(POS, D).astype(F32)).astype(BF)]
  transfers between devices with their start and end apart: 13 -> 13, of which waited for: 9 -> 9; matrix products, arithmetic and copies ran while one was open for 9% -> 2% of each run, Pallas kernels for 16% -> 21%
where the time goes in v2:
time: 250 us; the launch traced here: 249 us
  waiting for transfers between devices  78.5 us (31%)
  starting transfers between devices  61 us (24%)
  Pallas kernels  57.5 us (23%)
  blocking collectives  29.3 us (12%)
  between operations  14.2 us (6%)
  other arithmetic  4.43 us (2%)
  local copies, waits for them, and re-layouts  3.78 us (2%)
    all_to_all x5, waiting for transfers between devices, exchange(): lax.all_to_all(blocks, axis, 0, 0, axis_index_groups=groups, tiled=True)  56.8 us
    all_to_all x5, starting transfers between devices, exchange(): lax.all_to_all(blocks, axis, 0, 0, axis_index_groups=groups, tiled=True)  42.3 us
    all_to_all x1, blocking collectives, exchange(): lax.all_to_all(blocks, axis, 0, 0, axis_index_groups=groups, tiled=True)  29.3 us
    pallas_call x1, Pallas kernels, backward(): pl.pallas_call(backward_kernel, grid=(STEPS,), in_specs=[pl.BlockSpec(mem...  23.5 us
    pallas_call x1, Pallas kernels, forward(): pl.pallas_call(forward_kernel, grid=(STEPS,), in_specs=[pl.BlockSpec((SEQ...  15.8 us
    ppermute x3, waiting for transfers between devices, body(): out_blocks[r] = lax.ppermute(out_blocks[r], 'dp', route)  14.4 us
    pallas_call x1, Pallas kernels, output(): pl.pallas_call(output_kernel, grid=(POS // ROWS,), in_specs=[pl.BlockSpec...  8.08 us
    ppermute x3, starting transfers between devices, body(): out_blocks[r] = lax.ppermute(out_blocks[r], 'dp', route)  5.28 us
  transfers between devices with their start and end apart: 13, of which 9 were waited for; matrix products, arithmetic and copies ran while one was open for 2% of the time, Pallas kernels for 21%

profile of v2, /device:TPU:1, one launch (start us, length us, event | category | flops | bytes accessed | tf_op | source)
XLA Modules:
  0.0 248.7 jit_solution(7104304699814764332)
XLA Ops:
  7.2 0.0 copy-start.8
  7.2 0.0 copy-start.9
  7.2 10.2 %all-to-all-start = ((bf16[16,48,1152]{2,1,0:T(8,128)(2,1)}), bf16[16,48,1152]{2,1,0:T(8,128)(2,1)S(1)}, u32[]{:S(2)}, u32[]{:S(2)}) async-start(bf16[16,48,1152]{2,1,0:T(8,128)(2,1)} %bitcast.17), calls=%async_computation | async-start | bytes 3538944 | tf_op jit(solution)/shard_map/all_to_all | solution.py:488
  17.4 0.0 copy-done.8
  17.4 0.0 copy-done.9
  17.4 0.6 bitcast_add_fusion.mod_ref
  18.0 4.9 %grad_mixed.1 = bf16[768,576]{1,0:T(8,128)(2,1)} custom-call(bf16[768,1152]{1,0:T(8,128)(2,1)} %bitcast.14, f32[3,1152]{1,0:T(4,128)} %bitcast_add_fusion.mod_ref, bf16[576,1152]{1,0:T(8,128)(2,1)} %w_ref.3), custom_call_target="tpu_custom_call" | custom-call | flops 1019215872 | bytes 4000000 | tf_op jit(solution)/shard_map/grad_mixed/pallas_call | solution.py:151
  22.9 34.9 %all-to-all-done.x_ref = bf16[16,48,1152]{2,1,0:T(8,128)(2,1)S(1)} async-done(((bf16[16,48,1152]{2,1,0:T(8,128)(2,1)}), bf16[16,48,1152]{2,1,0:T(8,128)(2,1)S(1)}, u32[]{:S(2)}, u32[]{:S(2)}) %all-to-all-start) | async-done | bytes 1769504 | tf_op jit(solution)/shard_map/all_to_all | solution.py:488
  57.7 0.0 copy-start.5
  57.7 6.8 %all-to-all-start.1 = ((bf16[16,48,576]{2,1,0:T(8,128)(2,1)}), bf16[16,48,576]{2,1,0:T(8,128)(2,1)S(1)}, u32[]{:S(2)}, u32[]{:S(2)}) async-start(bf16[16,48,576]{2,1,0:T(8,128)(2,1)} %bitcast.16), calls=%async_computation.1 | async-start | bytes 1966080 | tf_op jit(solution)/shard_map/all_to_all | solution.py:488
  64.5 0.0 copy-done.5
  64.5 15.8 %forward.1 = (bf16[768,1728]{1,0:T(8,128)(2,1)}, bf16[16,48,576]{2,1,0:T(8,128)(2,1)}) custom-call(bf16[16,48,1152]{2,1,0:T(8,128)(2,1)} %copy-done.5, f32[3,1152]{1,0:T(4,128)} %bitcast_add_fusion.mod_ref, bf16[1728,1152]{1,0:T(8,128)(2,1)} %bitcast.20), custom_call_target="tpu_custom_call" | custom-call | flops 6115295232 | bytes 12000000 | tf_op jit(solution)/shard_map/forward/pallas_call | solution.py:121
  80.3 8.3 %all-to-all-done.1.gm_ref = bf16[16,48,576]{2,1,0:T(8,128)(2,1)S(1)} async-done(((bf16[16,48,576]{2,1,0:T(8,128)(2,1)}), bf16[16,48,576]{2,1,0:T(8,128)(2,1)S(1)}, u32[]{:S(2)}, u32[]{:S(2)}) %all-to-all-start.1) | async-done | bytes 884768 | tf_op jit(solution)/shard_map/all_to_all | solution.py:488
  88.5 0.0 copy-start.7
  88.5 6.2 %all-to-all-start.2 = ((bf16[16,48,576]{2,1,0:T(8,128)(2,1)}), bf16[16,48,576]{2,1,0:T(8,128)(2,1)S(1)}, u32[]{:S(2)}, u32[]{:S(2)}) async-start(bf16[16,48,576]{2,1,0:T(8,128)(2,1)} %get-tuple-element.33), calls=%async_computation.2 | async-start | bytes 1966080 | tf_op jit(solution)/shard_map/all_to_all | solution.py:488
  94.8 0.0 reduce-scatter.2.cloned.1.call-start
  94.8 0.7 pad_add_fusion.place_ref
  95.5 0.0 copy-done.7
  95.5 23.5 %backward.1 = (bf16[16,48,1152]{2,1,0:T(8,128)(2,1)}, bf16[8,72,1728]{2,1,0:T(8,128)(2,1)}, bf16[8,72,1728]{2,1,0:T(8,128)(2,1)}, f32[8,1152]{1,0:T(8,128)}) custom-call(s32[3]{0:T(128)} %pad_add_fusion.place_ref, bf16[16,48,1152]{2,1,0:T(8,128)(2,1)} %copy-done.5, bf16[16,48,576]{2,1,0:T(8,128)(2,1)} %copy-done.7, ...), custom_call_target="tpu_custom_call" | custom-call | flops 12230590464 | bytes 20000000 | tf_op jit(solution)/shard_map/backward/pallas_call | solution.py:237
  119.0 0.0 all-to-all-done.2
  119.0 0.0 copy-start.6
  119.1 3.6 %collective-permute-start = (bf16[8,72,1728]{2,1,0:T(8,128)(2,1)}, bf16[8,72,1728]{2,1,0:T(8,128)(2,1)S(1)}, u32[]{:S(2)}, u32[]{:S(2)}) collective-permute-start(bf16[8,72,1728]{2,1,0:T(8,128)(2,1)} %get-tuple-element.37), channel_id=1, source_target_pairs={{0,16},{16,0},{32,48},{48,32},{64,80},{80,64},{96,112},{112,96},{1... | collective-permute-start | bytes 5971976 | tf_op jit(solution)/shard_map/ppermute | solution.py:508
  122.7 4.0 %collective-permute-done.got_ref = bf16[8,72,1728]{2,1,0:T(8,128)(2,1)S(1)} collective-permute-done((bf16[8,72,1728]{2,1,0:T(8,128)(2,1)}, bf16[8,72,1728]{2,1,0:T(8,128)(2,1)S(1)}, u32[]{:S(2)}, u32[]{:S(2)}) %collective-permute-start) | collective-permute-done | bytes 1990688 | tf_op jit(solution)/shard_map/ppermute | solution.py:508
  126.6 0.0 copy-start
  126.6 1.6 copy-done
  128.2 1.8 pair_sum.1
  130.0 0.0 copy-done.6
  130.0 0.0 reduce-scatter.2.cloned.1.call-update
  130.1 5.8 %all-to-all-start.3 = ((bf16[16,48,1152]{2,1,0:T(8,128)(2,1)}), bf16[16,48,1152]{2,1,0:T(8,128)(2,1)}, u32[]{:S(2)}, u32[]{:S(2)}) async-start(bf16[16,48,1152]{2,1,0:T(8,128)(2,1)} %get-tuple-element.46), calls=%async_computation.4 | async-start | bytes 3538944 | tf_op jit(solution)/shard_map/all_to_all | solution.py:488
  135.9 0.0 copy-start.3
  135.9 8.1 %output.1 = (bf16[768,1152]{1,0:T(8,128)(2,1)}, bf16[8,40,1152]{2,1,0:T(8,128)(2,1)}, bf16[8,40,1152]{2,1,0:T(8,128)(2,1)}) custom-call(s32[3]{0:T(128)} %pad_add_fusion.place_ref, bf16[768,576]{1,0:T(8,128)(2,1)} %bitcast.19, bf16[768,1152]{1,0:T(8,128)(2,1)} %bitcast.18, bf16[768,1152]{1,0:T(8,128)(2,1)} %bitcast.15, f32[3,1152]{1,0:T(4,128)} %bitcast_add_fusion.mod_ref, ...), custom_call_target="tpu_custom_call" | custom-call | flops 2038431744 | bytes 9000000 | tf_op jit(solution)/shard_map/output/pallas_call | solution.py:312
  143.9 0.6 collective-permute-start.1
  144.5 2.1 collective-permute-done.1.got_ref
  146.6 0.0 copy-done.3
  146.6 0.0 copy-start.1
  146.6 1.1 copy-done.1
  147.7 0.9 pair_turn.1
  148.6 1.6 collective-permute-start.2
  150.2 2.6 %collective-permute-start.3 = (bf16[2,40,1152]{2,1,0:T(8,128)(2,1)S(1)}, bf16[2,40,1152]{2,1,0:T(8,128)(2,1)S(1)}, u32[]{:S(2)}, u32[]{:S(2)}) collective-permute-start(bf16[2,40,1152]{2,1,0:T(8,128)(2,1)S(1)} %get-tuple-element.44), channel_id=1, source_target_pairs={{0,64},{16,80},{32,96},{48,112},{64,0},{80,16},{96,32},{112,48},{1... | collective-permute-start | bytes 552968 | tf_op jit(solution)/shard_map/ppermute | solution.py:519
  152.8 1.1 collective-permute-start.4
  153.9 7.0 %collective-permute-done.2.o1 = bf16[2,40,1152]{2,1,0:T(8,128)(2,1)S(1)} collective-permute-done((bf16[2,40,1152]{2,1,0:T(8,128)(2,1)S(1)}, bf16[2,40,1152]{2,1,0:T(8,128)(2,1)S(1)}, u32[]{:S(2)}, u32[]{:S(2)}) %collective-permute-start.2) | collective-permute-done | bytes 184352 | tf_op jit(solution)/shard_map/ppermute | solution.py:519
  160.9 7.4 %collective-permute-done.3.o2 = bf16[2,40,1152]{2,1,0:T(8,128)(2,1)S(1)} collective-permute-done((bf16[2,40,1152]{2,1,0:T(8,128)(2,1)S(1)}, bf16[2,40,1152]{2,1,0:T(8,128)(2,1)S(1)}, u32[]{:S(2)}, u32[]{:S(2)}) %collective-permute-start.3) | collective-permute-done | bytes 184352 | tf_op jit(solution)/shard_map/ppermute | solution.py:519
  168.4 0.0 collective-permute-done.4.o3
  168.4 0.0 reduce-scatter.2.cloned.1.call-done.qkv_ref
  168.4 0.0 copy-start.2
  168.4 1.0 copy-done.2
  169.4 0.2 block_pieces.1
  169.6 0.0 copy-start.4
  169.6 7.2 %all-to-all-done.3 = bf16[16,48,1152]{2,1,0:T(8,128)(2,1)} async-done(((bf16[16,48,1152]{2,1,0:T(8,128)(2,1)}), bf16[16,48,1152]{2,1,0:T(8,128)(2,1)}, u32[]{:S(2)}, u32[]{:S(2)}) %all-to-all-start.3) | async-done | bytes 1769504 | tf_op jit(solution)/shard_map/all_to_all | solution.py:488
  176.8 29.3 %all_to_all.30.pieces_ref = bf16[16,208,128]{2,1,0:T(8,128)(2,1)S(1)} all-to-all(bf16[16,208,128]{2,1,0:T(8,128)(2,1)S(1)} %block_pieces.1), channel_id=1, replica_groups=mesh['dp'=16,'seq'=16] {'seq'}, dimensions={0} | all-to-all | bytes 1703936 | tf_op jit(solution)/shard_map/all_to_all | solution.py:488
  206.1 0.7 seq_sum.1
  206.8 4.1 %collective-permute-start.5 = (f32[120,128]{1,0:T(8,128)S(1)}, f32[120,128]{1,0:T(8,128)S(1)}, u32[]{:S(2)}, u32[]{:S(2)}) collective-permute-start(f32[120,128]{1,0:T(8,128)S(1)} %get-tuple-element.49), channel_id=1, source_target_pairs={{0,0},{1,16},{2,32},{3,48},{4,64},{5,80},{6,96},{7,112},{8,128},{9... | collective-permute-start | bytes 184328 | tf_op jit(solution)/shard_map/ppermute | solution.py:526
  210.9 5.1 %collective-permute-start.6 = (f32[120,128]{1,0:T(8,128)S(1)}, f32[120,128]{1,0:T(8,128)S(1)}, u32[]{:S(2)}, u32[]{:S(2)}) collective-permute-start(f32[120,128]{1,0:T(8,128)S(1)} %get-tuple-element.50), channel_id=1, source_target_pairs={{0,8},{1,24},{2,40},{3,56},{4,72},{5,88},{6,104},{7,120},{8,136},{... | collective-permute-start | bytes 184328 | tf_op jit(solution)/shard_map/ppermute | solution.py:527
  216.0 0.0 collective-permute-done.5.own_ref
  216.0 1.3 collective-permute-done.6.other_ref
  217.3 0.8 last_sum.1
  218.1 13.4 %all-to-all-start.5 = ((bf16[16,88,128]{2,1,0:T(8,128)(2,1)}), bf16[16,88,128]{2,1,0:T(8,128)(2,1)S(1)}, u32[]{:S(2)}, u32[]{:S(2)}) async-start(bf16[16,88,128]{2,1,0:T(8,128)(2,1)} %get-tuple-element.51), calls=%async_computation.6 | async-start | bytes 720896 | tf_op jit(solution)/shard_map/all_to_all | solution.py:488
  231.4 0.0 copy-done.4
  231.5 3.1 %fusion = bf16[1,1,768,1152]{3,2,1,0:T(8,128)(2,1)} fusion(bf16[1,1,768,1152]{3,2,1,0:T(8,128)(2,1)} %bitcast.11, bf16[1,1,768,1152]{3,2,1,0:T(8,128)(2,1)S(1)} %copy-done.4), kind=kLoop, calls=%fused_computation.1 | loop fusion | flops 3538944 | bytes 5308416 | tf_op jit(solution)/shard_map/convert_element_type | solution.py:530
  234.6 6.4 %all-to-all-done.5.pieces_ref = bf16[16,88,128]{2,1,0:T(8,128)(2,1)S(1)} async-done(((bf16[16,88,128]{2,1,0:T(8,128)(2,1)}), bf16[16,88,128]{2,1,0:T(8,128)(2,1)S(1)}, u32[]{:S(2)}, u32[]{:S(2)}) %all-to-all-start.5) | async-done | bytes 360480 | tf_op jit(solution)/shard_map/all_to_all | solution.py:488
  241.0 0.9 assemble.1
Async XLA Ops:
  7.2 10.2 %copy-start.8 = (f32[3,1152]{1,0:T(4,128)S(1)}, f32[3,1152]{1,0:T(4,128)}, u32[]{:S(2)}) copy-start(f32[3,1152]{1,0:T(4,128)} %param.8) | copy-start | bytes 41476
  7.2 10.2 %copy-start.9 = (f32[1,3,1152]{2,0,1:T(1,128)S(1)}, f32[1,3,1152]{2,0,1:T(1,128)}, u32[]{:S(2)}) copy-start(f32[1,3,1152]{2,0,1:T(1,128)} %param.7) | copy-start | bytes 41476
  7.2 50.6 %all-to-all-start = ((bf16[16,48,1152]{2,1,0:T(8,128)(2,1)}), bf16[16,48,1152]{2,1,0:T(8,128)(2,1)S(1)}, u32[]{:S(2)}, u32[]{:S(2)}) async-start(bf16[16,48,1152]{2,1,0:T(8,128)(2,1)} %bitcast.17), calls=%async_computation | async-start | bytes 3538944 | tf_op jit(solution)/shard_map/all_to_all | solution.py:488
  57.7 6.8 %copy-start.5 = (bf16[16,48,1152]{2,1,0:T(8,128)(2,1)}, bf16[16,48,1152]{2,1,0:T(8,128)(2,1)S(1)}, u32[]{:S(2)}) copy-start(bf16[16,48,1152]{2,1,0:T(8,128)(2,1)S(1)} %all-to-all-done.x_ref) | copy-start | bytes 5308420
  57.7 30.8 %all-to-all-start.1 = ((bf16[16,48,576]{2,1,0:T(8,128)(2,1)}), bf16[16,48,576]{2,1,0:T(8,128)(2,1)S(1)}, u32[]{:S(2)}, u32[]{:S(2)}) async-start(bf16[16,48,576]{2,1,0:T(8,128)(2,1)} %bitcast.16), calls=%async_computation.1 | async-start | bytes 1966080 | tf_op jit(solution)/shard_map/all_to_all | solution.py:488
  88.5 7.0 %copy-start.7 = (bf16[16,48,576]{2,1,0:T(8,128)(2,1)}, bf16[16,48,576]{2,1,0:T(8,128)(2,1)S(1)}, u32[]{:S(2)}) copy-start(bf16[16,48,576]{2,1,0:T(8,128)(2,1)S(1)} %all-to-all-done.1.gm_ref) | copy-start | bytes 2654212
  88.5 30.5 %all-to-all-start.2 = ((bf16[16,48,576]{2,1,0:T(8,128)(2,1)}), bf16[16,48,576]{2,1,0:T(8,128)(2,1)S(1)}, u32[]{:S(2)}, u32[]{:S(2)}) async-start(bf16[16,48,576]{2,1,0:T(8,128)(2,1)} %get-tuple-element.33), calls=%async_computation.2 | async-start | bytes 1966080 | tf_op jit(solution)/shard_map/all_to_all | solution.py:488
  94.8 73.6 %reduce-scatter.2.cloned.1.call-start = ((), (), s32[]{:S(2)}) async-start(), calls=%async_computation.7 | async-start | bytes 2580480 | tf_op jit(solution)/shard_map/reduce_scatter | solution.py:510
  119.0 11.0 %copy-start.6 = (bf16[16,48,576]{2,1,0:T(8,128)(2,1)}, bf16[16,48,576]{2,1,0:T(8,128)(2,1)S(1)}, u32[]{:S(2)}) copy-start(bf16[16,48,576]{2,1,0:T(8,128)(2,1)S(1)} %all-to-all-done.2) | copy-start | bytes 2654212
  119.1 7.6 %collective-permute-start = (bf16[8,72,1728]{2,1,0:T(8,128)(2,1)}, bf16[8,72,1728]{2,1,0:T(8,128)(2,1)S(1)}, u32[]{:S(2)}, u32[]{:S(2)}) collective-permute-start(bf16[8,72,1728]{2,1,0:T(8,128)(2,1)} %get-tuple-element.37), channel_id=1, source_target_pairs={{0,16},{16,0},{32,48},{48,32},{64,80},{80,64},{96,112},{112,96},{1... | collective-permute-start | bytes 5971976 | tf_op jit(solution)/shard_map/ppermute | solution.py:508
  126.6 1.6 copy-start
  130.1 46.8 %all-to-all-start.3 = ((bf16[16,48,1152]{2,1,0:T(8,128)(2,1)}), bf16[16,48,1152]{2,1,0:T(8,128)(2,1)}, u32[]{:S(2)}, u32[]{:S(2)}) async-start(bf16[16,48,1152]{2,1,0:T(8,128)(2,1)} %get-tuple-element.46), calls=%async_computation.4 | async-start | bytes 3538944 | tf_op jit(solution)/shard_map/all_to_all | solution.py:488
  135.9 10.7 %copy-start.3 = (s32[3]{0:T(128)S(1)}, s32[3]{0:T(128)}, u32[]{:S(2)}) copy-start(s32[3]{0:T(128)} %pad_add_fusion.place_ref) | copy-start | bytes 40
  143.9 2.6 %collective-permute-start.1 = (bf16[8,40,1152]{2,1,0:T(8,128)(2,1)}, bf16[8,40,1152]{2,1,0:T(8,128)(2,1)S(1)}, u32[]{:S(2)}, u32[]{:S(2)}) collective-permute-start(bf16[8,40,1152]{2,1,0:T(8,128)(2,1)} %get-tuple-element.41), channel_id=1, source_target_pairs={{0,16},{16,0},{32,48},{48,32},{64,80},{80,64},{96,112},{112,96},{1... | collective-permute-start | bytes 2211848 | tf_op jit(solution)/shard_map/ppermute | solution.py:516
  146.6 1.1 copy-start.1
  148.6 12.3 %collective-permute-start.2 = (bf16[2,40,1152]{2,1,0:T(8,128)(2,1)S(1)}, bf16[2,40,1152]{2,1,0:T(8,128)(2,1)S(1)}, u32[]{:S(2)}, u32[]{:S(2)}) collective-permute-start(bf16[2,40,1152]{2,1,0:T(8,128)(2,1)S(1)} %get-tuple-element.43), channel_id=1, source_target_pairs={{0,32},{16,48},{32,64},{48,80},{64,96},{80,112},{96,0},{112,16},{1... | collective-permute-start | bytes 552968 | tf_op jit(solution)/shard_map/ppermute | solution.py:519
  150.2 18.2 %collective-permute-start.3 = (bf16[2,40,1152]{2,1,0:T(8,128)(2,1)S(1)}, bf16[2,40,1152]{2,1,0:T(8,128)(2,1)S(1)}, u32[]{:S(2)}, u32[]{:S(2)}) collective-permute-start(bf16[2,40,1152]{2,1,0:T(8,128)(2,1)S(1)} %get-tuple-element.44), channel_id=1, source_target_pairs={{0,64},{16,80},{32,96},{48,112},{64,0},{80,16},{96,32},{112,48},{1... | collective-permute-start | bytes 552968 | tf_op jit(solution)/shard_map/ppermute | solution.py:519
  152.8 15.5 %collective-permute-start.4 = (bf16[2,40,1152]{2,1,0:T(8,128)(2,1)S(1)}, bf16[2,40,1152]{2,1,0:T(8,128)(2,1)S(1)}, u32[]{:S(2)}, u32[]{:S(2)}) collective-permute-start(bf16[2,40,1152]{2,1,0:T(8,128)(2,1)S(1)} %get-tuple-element.45), channel_id=1, source_target_pairs={{0,96},{16,112},{32,0},{48,16},{64,32},{80,48},{96,64},{112,80},{1... | collective-permute-start | bytes 552968 | tf_op jit(solution)/shard_map/ppermute | solution.py:519
  168.4 1.0 copy-start.2
  169.6 61.9 %copy-start.4 = (bf16[1,1,768,1152]{3,2,1,0:T(8,128)(2,1)S(1)}, bf16[1,1,768,1152]{3,2,1,0:T(8,128)(2,1)}, u32[]{:S(2)}) copy-start(bf16[1,1,768,1152]{3,2,1,0:T(8,128)(2,1)} %param.11) | copy-start | bytes 5308420
  206.8 9.2 %collective-permute-start.5 = (f32[120,128]{1,0:T(8,128)S(1)}, f32[120,128]{1,0:T(8,128)S(1)}, u32[]{:S(2)}, u32[]{:S(2)}) collective-permute-start(f32[120,128]{1,0:T(8,128)S(1)} %get-tuple-element.49), channel_id=1, source_target_pairs={{0,0},{1,16},{2,32},{3,48},{4,64},{5,80},{6,96},{7,112},{8,128},{9... | collective-permute-start | bytes 184328 | tf_op jit(solution)/shard_map/ppermute | solution.py:526
  210.9 6.4 %collective-permute-start.6 = (f32[120,128]{1,0:T(8,128)S(1)}, f32[120,128]{1,0:T(8,128)S(1)}, u32[]{:S(2)}, u32[]{:S(2)}) collective-permute-start(f32[120,128]{1,0:T(8,128)S(1)} %get-tuple-element.50), channel_id=1, source_target_pairs={{0,8},{1,24},{2,40},{3,56},{4,72},{5,88},{6,104},{7,120},{8,136},{... | collective-permute-start | bytes 184328 | tf_op jit(solution)/shard_map/ppermute | solution.py:527
  218.1 22.9 %all-to-all-start.5 = ((bf16[16,88,128]{2,1,0:T(8,128)(2,1)}), bf16[16,88,128]{2,1,0:T(8,128)(2,1)S(1)}, u32[]{:S(2)}, u32[]{:S(2)}) async-start(bf16[16,88,128]{2,1,0:T(8,128)(2,1)} %get-tuple-element.51), calls=%async_computation.6 | async-start | bytes 720896 | tf_op jit(solution)/shard_map/all_to_all | solution.py:488
Sparse Core Ops, SparseCore 0:
  130.2 36.5 reduce-scatter.1

commit v3 on v2

--- a/solution.py
+++ b/solution.py
@@ -167,8 +167,8 @@
 
 
 def backward_kernel(
-    place_ref, x_ref, gm_ref, packed_ref, mod_ref, w_ref,
-    delta_ref, keep_ref, send_ref, table_ref,
+    x_ref, gm_ref, packed_ref, mod_ref, w_ref,
+    delta_ref, blocks_ref, table_ref,
     modulated_all, gp_all, total,
 ):
     step = pl.program_id(0)
@@ -222,23 +222,17 @@
         for r in range(3):
             part = slice(r * 384, r * 384 + 384)
             total[part, :] = dot(modulated_all[:, part], gp_all[...], TN)
-        core = place_ref[0]
         rows = D // DP
-        for k in range(CHIPS):
-            chip = k % 2 * 4 + k // 2
-            mine = pl.multiple_of((2 * chip + core) * rows, 8)
-            other = pl.multiple_of((2 * chip + 1 - core) * rows, 8)
-            keep_ref[k] = total[pl.ds(mine, rows), :].astype(BF)
-            send_ref[k] = total[pl.ds(other, rows), :].astype(BF)
-
-
-def backward(place, x, grad_mixed, packed, modulation, w_turned):
-    half = jax.ShapeDtypeStruct((CHIPS, D // DP, 3 * INNER), BF)
+        for i in range(DP):
+            blocks_ref[i % 8 * 2 + i // 8] = total[rows * i : rows * i + rows, :].astype(BF)
+
+
+def backward(x, grad_mixed, packed, modulation, w_turned):
+    blocks = jax.ShapeDtypeStruct((DP, D // DP, 3 * INNER), BF)
     return pl.pallas_call(
         backward_kernel,
         grid=(STEPS,),
         in_specs=[
-            pl.BlockSpec(memory_space=pltpu.SMEM),
             pl.BlockSpec((SEQ, TILE, D), lambda j: (0, j, 0)),
             pl.BlockSpec((SEQ, TILE, INNER), lambda j: (0, j, 0)),
             pl.BlockSpec((ROWS, 3 * INNER), lambda j: (j, 0)),
@@ -247,14 +241,12 @@
         ],
         out_specs=[
             pl.BlockSpec((SEQ, TILE, D), lambda j: (0, j, 0)),
-            pl.BlockSpec(half.shape, lambda j: (0, 0, 0)),
-            pl.BlockSpec(half.shape, lambda j: (0, 0, 0)),
+            pl.BlockSpec(blocks.shape, lambda j: (0, 0, 0)),
             pl.BlockSpec((8, D), lambda j: (0, 0)),
         ],
         out_shape=[
             jax.ShapeDtypeStruct((SEQ, HERE, D), BF),
-            half,
-            half,
+            blocks,
             jax.ShapeDtypeStruct((8, D), F32),
         ],
         scratch_shapes=[
@@ -267,7 +259,7 @@
             flops=2 * POS * D * 3 * INNER * 4, bytes_accessed=20_000_000, transcendentals=800_000
         ),
         name="backward",
-    )(place, x, grad_mixed, packed, modulation, w_turned)
+    )(x, grad_mixed, packed, modulation, w_turned)
 
 
 def output_kernel(
@@ -353,14 +345,6 @@
     )(*args)
 
 
-def pair_kernel(keep_ref, got_ref, out_ref):
-    out_ref[...] = (keep_ref[...].astype(F32) + got_ref[...].astype(F32)).astype(BF)
-
-
-def pair_sum(keep, got):
-    return whole_call(pair_kernel, "pair_sum", jax.ShapeDtypeStruct(keep.shape, BF), keep, got)
-
-
 def pair_turn_kernel(place_ref, keep_ref, got_ref, *refs):
     total = refs[4]
     total[...] = (keep_ref[...].astype(F32) + got_ref[...].astype(F32)).astype(BF)
@@ -401,20 +385,21 @@
 def pieces_kernel(qkv_ref, o0, o1, o2, o3, pieces_ref):
     parts = []
     for x in range(2):
-        out = sum(o[x].astype(F32) for o in (o0, o1, o2, o3))
+        out = (o0[x].astype(F32) + o2[x].astype(F32)) + (o1[x].astype(F32) + o3[x].astype(F32))
         parts.append(stacked(qkv_ref[x].astype(F32), SEQ * QKV_ROWS))
         parts.append(stacked(out[: INNER // DP], SEQ * OUT_ROWS))
     table = stacked(jnp.concatenate([out[INNER // DP :], jnp.zeros((4, D), F32)], axis=0)[:3], 32)
     for s in range(SEQ):
         rows = [p[h * s : h * s + h] for p, h in zip(parts, (QKV_ROWS, OUT_ROWS) * 2)]
-        pieces_ref[s] = jnp.concatenate(rows + [table], axis=0).astype(BF)
+        rows += [table[2 * s : 2 * s + 2], jnp.zeros((6, 128), F32)]
+        pieces_ref[s] = jnp.concatenate(rows, axis=0).astype(BF)
 
 
 def block_pieces(qkv_blocks, out_blocks):
     return whole_call(
         pieces_kernel,
         "block_pieces",
-        jax.ShapeDtypeStruct((SEQ, 2 * BLOCK_ROWS + 32, 128), BF),
+        jax.ShapeDtypeStruct((SEQ, 2 * BLOCK_ROWS + 8, 128), BF),
         qkv_blocks,
         *out_blocks,
     )
@@ -434,42 +419,37 @@
     return whole_call(
         functools.partial(seq_sum_kernel, factor),
         "seq_sum",
-        [jax.ShapeDtypeStruct((BLOCK_ROWS + 32, 128), F32)] * 2,
+        [jax.ShapeDtypeStruct((BLOCK_ROWS + 8, 128), F32)] * 2,
         place,
         pieces,
         smem=1,
     )
 
 
-def last_sum_kernel(own_ref, other_ref, pieces_ref, table_ref):
-    total = own_ref[...] + other_ref[...]
-    piece = total[:BLOCK_ROWS].astype(BF)
+def last_sum_kernel(own_ref, other_ref, pieces_ref):
+    piece = (own_ref[...] + other_ref[...]).astype(BF)
     for k in range(DP):
         pieces_ref[k] = piece
-    for r in range(3):
-        rows = [total[BLOCK_ROWS + 3 * c + r : BLOCK_ROWS + 3 * c + r + 1] for c in range(9)]
-        table_ref[r : r + 1, :] = jnp.concatenate(rows, axis=1)
 
 
 def last_sum(own, other):
     return whole_call(
         last_sum_kernel,
         "last_sum",
-        [
-            jax.ShapeDtypeStruct((DP, BLOCK_ROWS, 128), BF),
-            jax.ShapeDtypeStruct((3, D), F32),
-        ],
+        jax.ShapeDtypeStruct((DP, BLOCK_ROWS + 8, 128), BF),
         own,
         other,
     )
 
 
-def assemble_kernel(pieces_ref, qkv_ref, out_ref):
+def assemble_kernel(pieces_ref, qkv_ref, out_ref, table_ref):
     pieces = [pieces_ref[s].astype(F32) for s in range(DP)]
     qkv = jnp.concatenate([p[:QKV_ROWS] for p in pieces], axis=0)
-    out = jnp.concatenate([p[QKV_ROWS:] for p in pieces], axis=0)
+    out = jnp.concatenate([p[QKV_ROWS:BLOCK_ROWS] for p in pieces], axis=0)
+    table = jnp.concatenate([p[BLOCK_ROWS : BLOCK_ROWS + 2] for p in pieces], axis=0)
     qkv_ref[...] = unstacked(qkv, D // SEQ, 3 * INNER)
     out_ref[...] = unstacked(out, INNER // SEQ, D)
+    table_ref[...] = unstacked(table, 3, D)
 
 
 def assemble(pieces):
@@ -479,6 +459,7 @@
         [
             jax.ShapeDtypeStruct((D // SEQ, 3 * INNER), F32),
             jax.ShapeDtypeStruct((INNER // SEQ, D), F32),
+            jax.ShapeDtypeStruct((3, D), F32),
         ],
         pieces,
     )
@@ -499,20 +480,16 @@
     gm_pos = exchange(grad_mixed.reshape(SEQ, HERE, INNER), "seq")
     packed, mixed_pos = forward(x_pos, modulation, w_turned)
     mixed = exchange(mixed_pos, "seq").reshape(POS, INNER)
-    delta_pos, qkv_keep, qkv_send, table = backward(
-        place, x_pos, gm_pos, packed, modulation, w_turned
-    )
-    swap = [(i, i ^ 1) for i in range(DP)]
-    column = [[8 * x + 2 * y + c for y in range(4)] for x in range(2) for c in range(2)]
-    qkv_keep, qkv_send, mixed = lax.optimization_barrier((qkv_keep, qkv_send, mixed))
-    qkv_blocks = pair_sum(qkv_keep, lax.ppermute(qkv_send, "dp", swap))
-    table = lax.optimization_barrier((table, qkv_blocks))[0]
+    delta_pos, qkv_blocks, table = backward(x_pos, gm_pos, packed, modulation, w_turned)
+    column = [[8 * x + i for i in range(8)] for x in range(2)]
+    qkv_blocks, mixed = lax.optimization_barrier((qkv_blocks, mixed))
     qkv_blocks = lax.psum_scatter(
         qkv_blocks, "dp", scatter_dimension=0, axis_index_groups=column, tiled=True
     )
     out_tokens, out_keep, out_send = output(
         place, mixed, tokens, grad_rows, modulation, w_out, table
     )
+    swap = [(i, i ^ 1) for i in range(DP)]
     out_blocks = list(pair_turn(place, out_keep, lax.ppermute(out_send, "dp", swap)))
     for r in range(1, 4):
         route = [(i, i // 8 * 8 + (i + 2 * r) % 8) for i in range(DP)]
@@ -525,8 +502,8 @@
     turn_other = [(i * SEQ + s, s * SEQ + (i ^ 8)) for i in range(DP) for s in range(SEQ)]
     own = lax.ppermute(own, ("dp", "seq"), turn)
     other = lax.ppermute(other, ("dp", "seq"), turn_other)
-    pieces, table = last_sum(own, other)
-    qkv_grad, out_weight_grad = assemble(exchange(pieces, "dp"))
+    pieces = exchange(last_sum(own, other), "dp")
+    qkv_grad, out_weight_grad, table = assemble(pieces)
     grad_tokens = (grad_rows.astype(F32) + delta.reshape(POS, D).astype(F32)).astype(BF)
     return (
         out_tokens[None, None],

time: 250 us -> 238 us (0.952)
  waiting for transfers between devices: 78.5 us -> 75 us
  blocking collectives: 29.3 us -> 26.4 us
    reduce_scatter x1, waiting for transfers between devices: 0.01 us -> 8 us  [body(): lax.psum_scatter(qkv_blocks, 'dp', scatter_dimension=0, axis_index_groups...]
    all_to_all x5, waiting for transfers between devices: 56.8 us -> 50.4 us  [exchange(): lax.all_to_all(blocks, axis, 0, 0, axis_index_groups=groups, tiled=True)]
    ppermute x1 -> x0, waiting for transfers between devices: 3.95 us -> none  [body(): qkv_blocks = pair_sum(qkv_keep, lax.ppermute(qkv_send, 'dp', swap))]
    ppermute x1 -> x0, starting transfers between devices: 3.64 us -> none  [body(): qkv_blocks = pair_sum(qkv_keep, lax.ppermute(qkv_send, 'dp', swap))]
    all_to_all x1, blocking collectives: 29.3 us -> 26.4 us  [exchange(): lax.all_to_all(blocks, axis, 0, 0, axis_index_groups=groups, tiled=True)]
    ppermute x1, starting transfers between devices: 4.11 us -> 6.99 us  [body(): own = lax.ppermute(own, ('dp', 'seq'), turn)]
    ppermute x1, starting transfers between devices: 5.08 us -> 2.27 us  [body(): other = lax.ppermute(other, ('dp', 'seq'), turn_other)]
    ppermute x3, waiting for transfers between devices: 14.4 us -> 11.7 us  [body(): out_blocks[r] = lax.ppermute(out_blocks[r], 'dp', route)]
  transfers between devices with their start and end apart: 13 -> 12, of which waited for: 9 -> 9; matrix products, arithmetic and copies ran while one was open for 2% -> 2% of each run, Pallas kernels for 21% -> 22%
where the time goes in v3:
time: 238 us; the launch traced here: 237 us
  waiting for transfers between devices  75 us (32%)
  starting transfers between devices  59 us (25%)
  Pallas kernels  55.4 us (23%)
  blocking collectives  26.4 us (11%)
  between operations  14.2 us (6%)
  other arithmetic  4.36 us (2%)
  local copies, waits for them, and re-layouts  3.12 us (1%)
    all_to_all x5, waiting for transfers between devices, exchange(): lax.all_to_all(blocks, axis, 0, 0, axis_index_groups=groups, tiled=True)  50.4 us
    all_to_all x5, starting transfers between devices, exchange(): lax.all_to_all(blocks, axis, 0, 0, axis_index_groups=groups, tiled=True)  43.1 us
    all_to_all x1, blocking collectives, exchange(): lax.all_to_all(blocks, axis, 0, 0, axis_index_groups=groups, tiled=True)  26.4 us
    pallas_call x1, Pallas kernels, backward(): pl.pallas_call(backward_kernel, grid=(STEPS,), in_specs=[pl.BlockSpec((SE...  23.2 us
    pallas_call x1, Pallas kernels, forward(): pl.pallas_call(forward_kernel, grid=(STEPS,), in_specs=[pl.BlockSpec((SEQ...  15.8 us
    ppermute x3, waiting for transfers between devices, body(): out_blocks[r] = lax.ppermute(out_blocks[r], 'dp', route)  11.7 us
    pallas_call x1, Pallas kernels, output(): pl.pallas_call(output_kernel, grid=(POS // ROWS,), in_specs=[pl.BlockSpec...  8.12 us
    reduce_scatter x1, waiting for transfers between devices, body(): lax.psum_scatter(qkv_blocks, 'dp', scatter_dimension=0, axis_index_groups...  8 us
  transfers between devices with their start and end apart: 12, of which 9 were waited for; matrix products, arithmetic and copies ran while one was open for 2% of the time, Pallas kernels for 22%

profile of v3, /device:TPU:1, one launch (start us, length us, event | category | flops | bytes accessed | tf_op | source)
XLA Modules:
  0.0 237.5 jit_solution(7825165441353032840)
XLA Ops:
  7.2 0.0 copy-start.7
  7.2 0.0 copy-start.8
  7.2 10.2 %all-to-all-start = ((bf16[16,48,1152]{2,1,0:T(8,128)(2,1)}), bf16[16,48,1152]{2,1,0:T(8,128)(2,1)S(1)}, u32[]{:S(2)}, u32[]{:S(2)}) async-start(bf16[16,48,1152]{2,1,0:T(8,128)(2,1)} %bitcast.17), calls=%async_computation | async-start | bytes 3538944 | tf_op jit(solution)/shard_map/all_to_all | solution.py:469
  17.4 0.0 copy-done.7
  17.4 0.0 copy-done.8
  17.4 0.6 bitcast_add_fusion.mod_ref
  18.0 4.9 %grad_mixed.1 = bf16[768,576]{1,0:T(8,128)(2,1)} custom-call(bf16[768,1152]{1,0:T(8,128)(2,1)} %bitcast.14, f32[3,1152]{1,0:T(4,128)} %bitcast_add_fusion.mod_ref, bf16[576,1152]{1,0:T(8,128)(2,1)} %w_ref.3), custom_call_target="tpu_custom_call" | custom-call | flops 1019215872 | bytes 4000000 | tf_op jit(solution)/shard_map/grad_mixed/pallas_call | solution.py:151
  22.9 34.8 %all-to-all-done.x_ref = bf16[16,48,1152]{2,1,0:T(8,128)(2,1)S(1)} async-done(((bf16[16,48,1152]{2,1,0:T(8,128)(2,1)}), bf16[16,48,1152]{2,1,0:T(8,128)(2,1)S(1)}, u32[]{:S(2)}, u32[]{:S(2)}) %all-to-all-start) | async-done | bytes 1769504 | tf_op jit(solution)/shard_map/all_to_all | solution.py:469
  57.7 0.0 copy-start.4
  57.7 6.8 %all-to-all-start.1 = ((bf16[16,48,576]{2,1,0:T(8,128)(2,1)}), bf16[16,48,576]{2,1,0:T(8,128)(2,1)S(1)}, u32[]{:S(2)}, u32[]{:S(2)}) async-start(bf16[16,48,576]{2,1,0:T(8,128)(2,1)} %bitcast.16), calls=%async_computation.1 | async-start | bytes 1966080 | tf_op jit(solution)/shard_map/all_to_all | solution.py:469
  64.5 0.0 copy-done.4
  64.5 15.8 %forward.1 = (bf16[768,1728]{1,0:T(8,128)(2,1)}, bf16[16,48,576]{2,1,0:T(8,128)(2,1)}) custom-call(bf16[16,48,1152]{2,1,0:T(8,128)(2,1)} %copy-done.4, f32[3,1152]{1,0:T(4,128)} %bitcast_add_fusion.mod_ref, bf16[1728,1152]{1,0:T(8,128)(2,1)} %bitcast.20), custom_call_target="tpu_custom_call" | custom-call | flops 6115295232 | bytes 12000000 | tf_op jit(solution)/shard_map/forward/pallas_call | solution.py:121
  80.3 8.3 %all-to-all-done.1.gm_ref = bf16[16,48,576]{2,1,0:T(8,128)(2,1)S(1)} async-done(((bf16[16,48,576]{2,1,0:T(8,128)(2,1)}), bf16[16,48,576]{2,1,0:T(8,128)(2,1)S(1)}, u32[]{:S(2)}, u32[]{:S(2)}) %all-to-all-start.1) | async-done | bytes 884768 | tf_op jit(solution)/shard_map/all_to_all | solution.py:469
  88.5 0.0 copy-start.6
  88.5 6.2 %all-to-all-start.2 = ((bf16[16,48,576]{2,1,0:T(8,128)(2,1)}), bf16[16,48,576]{2,1,0:T(8,128)(2,1)S(1)}, u32[]{:S(2)}, u32[]{:S(2)}) async-start(bf16[16,48,576]{2,1,0:T(8,128)(2,1)} %get-tuple-element.28), calls=%async_computation.2 | async-start | bytes 1966080 | tf_op jit(solution)/shard_map/all_to_all | solution.py:469
  94.8 0.0 reduce-scatter.2.cloned.1.call-start
  94.8 0.0 copy-done.6
  94.8 23.2 %backward.1 = (bf16[16,48,1152]{2,1,0:T(8,128)(2,1)}, bf16[16,72,1728]{2,1,0:T(8,128)(2,1)}, f32[8,1152]{1,0:T(8,128)}) custom-call(bf16[16,48,1152]{2,1,0:T(8,128)(2,1)} %copy-done.4, bf16[16,48,576]{2,1,0:T(8,128)(2,1)} %copy-done.6, bf16[768,1728]{1,0:T(8,128)(2,1)} %get-tuple-element.26.packed_ref, f32[3,1152]{1,0:T(4,128)} %bitcast_add_fusion.mod_ref, ...), custom_call_target="tpu_custom_call" | custom-call | flops 12230590464 | bytes 20000000 | tf_op jit(solution)/shard_map/backward/pallas_call | solution.py:232
  118.0 0.5 all-to-all-done.2
  118.6 0.0 copy-start.5
  118.6 0.0 reduce-scatter.2.cloned.1.call-update
  118.6 0.9 copy-done.5
  119.5 7.1 %all-to-all-start.3 = ((bf16[16,48,1152]{2,1,0:T(8,128)(2,1)}), bf16[16,48,1152]{2,1,0:T(8,128)(2,1)}, u32[]{:S(2)}, u32[]{:S(2)}) async-start(bf16[16,48,1152]{2,1,0:T(8,128)(2,1)} %get-tuple-element.39), calls=%async_computation.4 | async-start | bytes 3538944 | tf_op jit(solution)/shard_map/all_to_all | solution.py:469
  126.6 0.6 pad_add_fusion.place_ref
  127.2 0.0 copy-start.2
  127.2 8.1 %output.1 = (bf16[768,1152]{1,0:T(8,128)(2,1)}, bf16[8,40,1152]{2,1,0:T(8,128)(2,1)}, bf16[8,40,1152]{2,1,0:T(8,128)(2,1)}) custom-call(s32[3]{0:T(128)} %pad_add_fusion.place_ref, bf16[768,576]{1,0:T(8,128)(2,1)} %bitcast.19, bf16[768,1152]{1,0:T(8,128)(2,1)} %bitcast.18, bf16[768,1152]{1,0:T(8,128)(2,1)} %bitcast.15, f32[3,1152]{1,0:T(4,128)} %bitcast_add_fusion.mod_ref, ...), custom_call_target="tpu_custom_call" | custom-call | flops 2038431744 | bytes 9000000 | tf_op jit(solution)/shard_map/output/pallas_call | solution.py:304
  135.4 1.7 collective-permute-start
  137.0 2.1 collective-permute-done.got_ref
  139.1 0.0 copy-done.2
  139.1 0.0 copy-start
  139.1 1.1 copy-done
  140.2 0.9 pair_turn.1
  141.2 1.3 collective-permute-start.1
  142.5 2.6 %collective-permute-start.2 = (bf16[2,40,1152]{2,1,0:T(8,128)(2,1)S(1)}, bf16[2,40,1152]{2,1,0:T(8,128)(2,1)S(1)}, u32[]{:S(2)}, u32[]{:S(2)}) collective-permute-start(bf16[2,40,1152]{2,1,0:T(8,128)(2,1)S(1)} %get-tuple-element.37), channel_id=1, source_target_pairs={{0,64},{16,80},{32,96},{48,112},{64,0},{80,16},{96,32},{112,48},{1... | collective-permute-start | bytes 552968 | tf_op jit(solution)/shard_map/ppermute | solution.py:496
  145.1 1.1 collective-permute-start.3
  146.2 4.8 %collective-permute-done.1.o1 = bf16[2,40,1152]{2,1,0:T(8,128)(2,1)S(1)} collective-permute-done((bf16[2,40,1152]{2,1,0:T(8,128)(2,1)S(1)}, bf16[2,40,1152]{2,1,0:T(8,128)(2,1)S(1)}, u32[]{:S(2)}, u32[]{:S(2)}) %collective-permute-start.1) | collective-permute-done | bytes 184352 | tf_op jit(solution)/shard_map/ppermute | solution.py:496
  151.0 6.9 %collective-permute-done.2.o2 = bf16[2,40,1152]{2,1,0:T(8,128)(2,1)S(1)} collective-permute-done((bf16[2,40,1152]{2,1,0:T(8,128)(2,1)S(1)}, bf16[2,40,1152]{2,1,0:T(8,128)(2,1)S(1)}, u32[]{:S(2)}, u32[]{:S(2)}) %collective-permute-start.2) | collective-permute-done | bytes 184352 | tf_op jit(solution)/shard_map/ppermute | solution.py:496
  157.9 0.0 collective-permute-done.3.o3
  157.9 8.0 %reduce-scatter.2.cloned.1.call-done.qkv_ref = bf16[2,72,1728]{2,1,0:T(8,128)(2,1)} async-done(((bf16[16,72,1728]{2,1,0:T(8,128)(2,1)}), bf16[2,72,1728]{2,1,0:T(8,128)(2,1)}) %reduce-scatter.2.cloned.1.call-update) | async-done | bytes 497680 | tf_op jit(solution)/shard_map/reduce_scatter | solution.py:486
  165.9 0.0 copy-start.1
  165.9 1.0 copy-done.1
  166.9 0.2 block_pieces.1
  167.1 0.0 copy-start.3
  167.1 0.0 all-to-all-done.3
  167.1 26.4 %all_to_all.30.pieces_ref = bf16[16,184,128]{2,1,0:T(8,128)(2,1)S(1)} all-to-all(bf16[16,184,128]{2,1,0:T(8,128)(2,1)S(1)} %block_pieces.1), channel_id=1, replica_groups=mesh['dp'=16,'seq'=16] {'seq'}, dimensions={0} | all-to-all | bytes 1507328 | tf_op jit(solution)/shard_map/all_to_all | solution.py:469
  193.5 0.7 seq_sum.1
  194.1 7.0 %collective-permute-start.4 = (f32[96,128]{1,0:T(8,128)S(1)}, f32[96,128]{1,0:T(8,128)S(1)}, u32[]{:S(2)}, u32[]{:S(2)}) collective-permute-start(f32[96,128]{1,0:T(8,128)S(1)} %get-tuple-element.42), channel_id=1, source_target_pairs={{0,0},{1,16},{2,32},{3,48},{4,64},{5,80},{6,96},{7,112},{8,128},{9... | collective-permute-start | bytes 147464 | tf_op jit(solution)/shard_map/ppermute | solution.py:503
  201.1 2.3 collective-permute-start.5
  203.4 0.0 collective-permute-done.4.own_ref
  203.4 2.8 %collective-permute-done.5.other_ref = f32[96,128]{1,0:T(8,128)S(1)} collective-permute-done((f32[96,128]{1,0:T(8,128)S(1)}, f32[96,128]{1,0:T(8,128)S(1)}, u32[]{:S(2)}, u32[]{:S(2)}) %collective-permute-start.5) | collective-permute-done | bytes 49184 | tf_op jit(solution)/shard_map/ppermute | solution.py:504
  206.3 0.8 last_sum.1
  207.0 12.8 %all-to-all-start.5 = ((bf16[16,96,128]{2,1,0:T(8,128)(2,1)}), bf16[16,96,128]{2,1,0:T(8,128)(2,1)S(1)}, u32[]{:S(2)}, u32[]{:S(2)}) async-start(bf16[16,96,128]{2,1,0:T(8,128)(2,1)} %last_sum.1), calls=%async_computation.6 | async-start | bytes 786432 | tf_op jit(solution)/shard_map/all_to_all | solution.py:469
  219.9 0.0 copy-done.3
  219.9 3.1 %fusion = bf16[1,1,768,1152]{3,2,1,0:T(8,128)(2,1)} fusion(bf16[1,1,768,1152]{3,2,1,0:T(8,128)(2,1)} %bitcast.11, bf16[1,1,768,1152]{3,2,1,0:T(8,128)(2,1)S(1)} %copy-done.3), kind=kLoop, calls=%fused_computation.1 | loop fusion | flops 3538944 | bytes 5308416 | tf_op jit(solution)/shard_map/convert_element_type | solution.py:507
  223.0 6.7 %all-to-all-done.5.pieces_ref = bf16[16,96,128]{2,1,0:T(8,128)(2,1)S(1)} async-done(((bf16[16,96,128]{2,1,0:T(8,128)(2,1)}), bf16[16,96,128]{2,1,0:T(8,128)(2,1)S(1)}, u32[]{:S(2)}, u32[]{:S(2)}) %all-to-all-start.5) | async-done | bytes 393248 | tf_op jit(solution)/shard_map/all_to_all | solution.py:469
  229.8 0.9 assemble.1
Async XLA Ops:
  7.2 10.2 %copy-start.7 = (f32[3,1152]{1,0:T(4,128)S(1)}, f32[3,1152]{1,0:T(4,128)}, u32[]{:S(2)}) copy-start(f32[3,1152]{1,0:T(4,128)} %param.8) | copy-start | bytes 41476
  7.2 10.2 %copy-start.8 = (f32[1,3,1152]{2,0,1:T(1,128)S(1)}, f32[1,3,1152]{2,0,1:T(1,128)}, u32[]{:S(2)}) copy-start(f32[1,3,1152]{2,0,1:T(1,128)} %param.7) | copy-start | bytes 41476
  7.2 50.6 %all-to-all-start = ((bf16[16,48,1152]{2,1,0:T(8,128)(2,1)}), bf16[16,48,1152]{2,1,0:T(8,128)(2,1)S(1)}, u32[]{:S(2)}, u32[]{:S(2)}) async-start(bf16[16,48,1152]{2,1,0:T(8,128)(2,1)} %bitcast.17), calls=%async_computation | async-start | bytes 3538944 | tf_op jit(solution)/shard_map/all_to_all | solution.py:469
  57.7 6.8 %copy-start.4 = (bf16[16,48,1152]{2,1,0:T(8,128)(2,1)}, bf16[16,48,1152]{2,1,0:T(8,128)(2,1)S(1)}, u32[]{:S(2)}) copy-start(bf16[16,48,1152]{2,1,0:T(8,128)(2,1)S(1)} %all-to-all-done.x_ref) | copy-start | bytes 5308420
  57.7 30.8 %all-to-all-start.1 = ((bf16[16,48,576]{2,1,0:T(8,128)(2,1)}), bf16[16,48,576]{2,1,0:T(8,128)(2,1)S(1)}, u32[]{:S(2)}, u32[]{:S(2)}) async-start(bf16[16,48,576]{2,1,0:T(8,128)(2,1)} %bitcast.16), calls=%async_computation.1 | async-start | bytes 1966080 | tf_op jit(solution)/shard_map/all_to_all | solution.py:469
  88.5 6.3 %copy-start.6 = (bf16[16,48,576]{2,1,0:T(8,128)(2,1)}, bf16[16,48,576]{2,1,0:T(8,128)(2,1)S(1)}, u32[]{:S(2)}) copy-start(bf16[16,48,576]{2,1,0:T(8,128)(2,1)S(1)} %all-to-all-done.1.gm_ref) | copy-start | bytes 2654212
  88.5 30.0 %all-to-all-start.2 = ((bf16[16,48,576]{2,1,0:T(8,128)(2,1)}), bf16[16,48,576]{2,1,0:T(8,128)(2,1)S(1)}, u32[]{:S(2)}, u32[]{:S(2)}) async-start(bf16[16,48,576]{2,1,0:T(8,128)(2,1)} %get-tuple-element.28), calls=%async_computation.2 | async-start | bytes 1966080 | tf_op jit(solution)/shard_map/all_to_all | solution.py:469
  94.8 71.1 %reduce-scatter.2.cloned.1.call-start = ((), (), s32[]{:S(2)}) async-start(), calls=%async_computation.7 | async-start | bytes 4644864 | tf_op jit(solution)/shard_map/reduce_scatter | solution.py:486
  118.6 0.9 copy-start.5
  119.5 47.6 %all-to-all-start.3 = ((bf16[16,48,1152]{2,1,0:T(8,128)(2,1)}), bf16[16,48,1152]{2,1,0:T(8,128)(2,1)}, u32[]{:S(2)}, u32[]{:S(2)}) async-start(bf16[16,48,1152]{2,1,0:T(8,128)(2,1)} %get-tuple-element.39), calls=%async_computation.4 | async-start | bytes 3538944 | tf_op jit(solution)/shard_map/all_to_all | solution.py:469
  127.2 11.9 %copy-start.2 = (s32[3]{0:T(128)S(1)}, s32[3]{0:T(128)}, u32[]{:S(2)}) copy-start(s32[3]{0:T(128)} %pad_add_fusion.place_ref) | copy-start | bytes 40
  135.4 3.7 %collective-permute-start = (bf16[8,40,1152]{2,1,0:T(8,128)(2,1)}, bf16[8,40,1152]{2,1,0:T(8,128)(2,1)S(1)}, u32[]{:S(2)}, u32[]{:S(2)}) collective-permute-start(bf16[8,40,1152]{2,1,0:T(8,128)(2,1)} %get-tuple-element.34), channel_id=1, source_target_pairs={{0,16},{16,0},{32,48},{48,32},{64,80},{80,64},{96,112},{112,96},{1... | collective-permute-start | bytes 2211848 | tf_op jit(solution)/shard_map/ppermute | solution.py:493
  139.1 1.1 copy-start
  141.2 9.8 %collective-permute-start.1 = (bf16[2,40,1152]{2,1,0:T(8,128)(2,1)S(1)}, bf16[2,40,1152]{2,1,0:T(8,128)(2,1)S(1)}, u32[]{:S(2)}, u32[]{:S(2)}) collective-permute-start(bf16[2,40,1152]{2,1,0:T(8,128)(2,1)S(1)} %get-tuple-element.36), channel_id=1, source_target_pairs={{0,32},{16,48},{32,64},{48,80},{64,96},{80,112},{96,0},{112,16},{1... | collective-permute-start | bytes 552968 | tf_op jit(solution)/shard_map/ppermute | solution.py:496
  142.5 15.3 %collective-permute-start.2 = (bf16[2,40,1152]{2,1,0:T(8,128)(2,1)S(1)}, bf16[2,40,1152]{2,1,0:T(8,128)(2,1)S(1)}, u32[]{:S(2)}, u32[]{:S(2)}) collective-permute-start(bf16[2,40,1152]{2,1,0:T(8,128)(2,1)S(1)} %get-tuple-element.37), channel_id=1, source_target_pairs={{0,64},{16,80},{32,96},{48,112},{64,0},{80,16},{96,32},{112,48},{1... | collective-permute-start | bytes 552968 | tf_op jit(solution)/shard_map/ppermute | solution.py:496
  145.1 12.7 %collective-permute-start.3 = (bf16[2,40,1152]{2,1,0:T(8,128)(2,1)S(1)}, bf16[2,40,1152]{2,1,0:T(8,128)(2,1)S(1)}, u32[]{:S(2)}, u32[]{:S(2)}) collective-permute-start(bf16[2,40,1152]{2,1,0:T(8,128)(2,1)S(1)} %get-tuple-element.38), channel_id=1, source_target_pairs={{0,96},{16,112},{32,0},{48,16},{64,32},{80,48},{96,64},{112,80},{1... | collective-permute-start | bytes 552968 | tf_op jit(solution)/shard_map/ppermute | solution.py:496
  165.9 1.0 copy-start.1
  167.1 52.8 %copy-start.3 = (bf16[1,1,768,1152]{3,2,1,0:T(8,128)(2,1)S(1)}, bf16[1,1,768,1152]{3,2,1,0:T(8,128)(2,1)}, u32[]{:S(2)}) copy-start(bf16[1,1,768,1152]{3,2,1,0:T(8,128)(2,1)} %param.11) | copy-start | bytes 5308420
  194.1 9.3 %collective-permute-start.4 = (f32[96,128]{1,0:T(8,128)S(1)}, f32[96,128]{1,0:T(8,128)S(1)}, u32[]{:S(2)}, u32[]{:S(2)}) collective-permute-start(f32[96,128]{1,0:T(8,128)S(1)} %get-tuple-element.42), channel_id=1, source_target_pairs={{0,0},{1,16},{2,32},{3,48},{4,64},{5,80},{6,96},{7,112},{8,128},{9... | collective-permute-start | bytes 147464 | tf_op jit(solution)/shard_map/ppermute | solution.py:503
  201.1 5.1 %collective-permute-start.5 = (f32[96,128]{1,0:T(8,128)S(1)}, f32[96,128]{1,0:T(8,128)S(1)}, u32[]{:S(2)}, u32[]{:S(2)}) collective-permute-start(f32[96,128]{1,0:T(8,128)S(1)} %get-tuple-element.43), channel_id=1, source_target_pairs={{0,8},{1,24},{2,40},{3,56},{4,72},{5,88},{6,104},{7,120},{8,136},{... | collective-permute-start | bytes 147464 | tf_op jit(solution)/shard_map/ppermute | solution.py:504
  207.0 22.7 %all-to-all-start.5 = ((bf16[16,96,128]{2,1,0:T(8,128)(2,1)}), bf16[16,96,128]{2,1,0:T(8,128)(2,1)S(1)}, u32[]{:S(2)}, u32[]{:S(2)}) async-start(bf16[16,96,128]{2,1,0:T(8,128)(2,1)} %last_sum.1), calls=%async_computation.6 | async-start | bytes 786432 | tf_op jit(solution)/shard_map/all_to_all | solution.py:469
Sparse Core Ops, SparseCore 0:
  118.7 47.0 reduce-scatter.1

commit v4 on v3

--- a/solution.py
+++ b/solution.py
@@ -15,16 +15,18 @@
 INNER = 576
 SEQ = 16
 DP = 16
-CHIPS = DP // 2
 HERE = POS // SEQ
 TILE = 16
 HALF = 8
 ROWS = SEQ * TILE
 UNIT = SEQ * HALF
 PAIR = 2 * HEAD_DIM
-QKV_ROWS = 64
-OUT_ROWS = 24
-BLOCK_ROWS = QKV_ROWS + OUT_ROWS
+CHUNKS = 8
+LANES = 256
+QKV_LANES = 3 * INNER // CHUNKS
+OUT_LANES = D // CHUNKS
+OUT_HEIGHT = INNER + 16
+PIECE_ROWS = 184
 STEPS = HERE // TILE
 EPSILON = 1e-06
 SCALE = 1.0 / math.sqrt(HEAD_DIM)
@@ -166,10 +168,15 @@
     )(out_grad, modulation, w_out)
 
 
+def chunk_of(rows, m, lanes):
+    pad = jnp.zeros((rows.shape[0], LANES - lanes), rows.dtype)
+    return jnp.concatenate([rows[:, lanes * m : lanes * m + lanes], pad], axis=1)
+
+
 def backward_kernel(
     x_ref, gm_ref, packed_ref, mod_ref, w_ref,
     delta_ref, blocks_ref, table_ref,
-    modulated_all, gp_all, total,
+    modulated_all, gp_all,
 ):
     step = pl.program_id(0)
     normed, inv_std = normalize(load_rows(x_ref[...]))
@@ -198,7 +205,8 @@
             pieces[2].append(gather(dot(flat(weights), grad_pair), first_wide).astype(BF))
         units.append(jnp.concatenate(pieces[0] + pieces[1] + pieces[2], axis=1))
     grad_packed = jnp.concatenate(units, axis=0)
-    gp_all[here, :] = grad_packed
+    for m in range(CHUNKS):
+        gp_all[here, LANES * m : LANES * m + LANES] = chunk_of(grad_packed, m, QKV_LANES)
     grad_mod = dot(grad_packed, w_ref[...])
     shift_sum = jnp.sum(grad_mod, axis=0, keepdims=True)
     scale_sum = jnp.sum(grad_mod * normed, axis=0, keepdims=True)
@@ -221,14 +229,13 @@
     def _():
         for r in range(3):
             part = slice(r * 384, r * 384 + 384)
-            total[part, :] = dot(modulated_all[:, part], gp_all[...], TN)
-        rows = D // DP
-        for i in range(DP):
-            blocks_ref[i % 8 * 2 + i // 8] = total[rows * i : rows * i + rows, :].astype(BF)
+            total = dot(modulated_all[:, part], gp_all[...], TN)
+            for m in range(CHUNKS):
+                blocks_ref[m, part, :] = total[:, LANES * m : LANES * m + LANES].astype(BF)
 
 
 def backward(x, grad_mixed, packed, modulation, w_turned):
-    blocks = jax.ShapeDtypeStruct((DP, D // DP, 3 * INNER), BF)
+    blocks = jax.ShapeDtypeStruct((CHUNKS, D, LANES), BF)
     return pl.pallas_call(
         backward_kernel,
         grid=(STEPS,),
@@ -251,8 +258,7 @@
         ],
         scratch_shapes=[
             pltpu.VMEM((POS, D), BF),
-            pltpu.VMEM((POS, 3 * INNER), BF),
-            pltpu.VMEM((D, 3 * INNER), F32),
+            pltpu.VMEM((POS, CHUNKS * LANES), BF),
         ],
         compiler_params=PARAMS,
         cost_estimate=pl.CostEstimate(
@@ -273,7 +279,9 @@
     out_ref[...] = (x_ref[...].astype(F32) + gate_row * branch).astype(BF)
     grad_out = grad_ref[...].astype(F32)
     gate_sum = jnp.sum(grad_out * branch, axis=0, keepdims=True)
-    term = dot(mixed, (grad_out * gate_row).astype(BF), TN)
+    grad_branch = (grad_out * gate_row).astype(BF)
+    chunks = [chunk_of(grad_branch, m, OUT_LANES) for m in range(CHUNKS)]
+    term = dot(mixed, jnp.concatenate(chunks, axis=1), TN)
 
     @pl.when(step == 0)
     def _():
@@ -285,22 +293,21 @@
 
     @pl.when(step == POS // ROWS - 1)
     def _():
-        rows = INNER // DP
-        core = place_ref[0]
         table = jnp.concatenate(
-            [table_ref[0:2, :], gate_total[0:1, :], jnp.zeros((1, D), F32)], axis=0
+            [table_ref[0:2, :], gate_total[0:1, :], jnp.zeros((13, D), F32)], axis=0
         )
-        for k in range(CHIPS):
-            chip = k % 2 * 4 + k // 2
-            both = total[2 * chip * rows : 2 * (chip + 1) * rows, :]
-            first = jnp.concatenate([both[:rows], table], axis=0).astype(BF)
-            second = jnp.concatenate([both[rows:], table], axis=0).astype(BF)
-            keep_ref[k] = jnp.where(core == 0, first, second)
-            send_ref[k] = jnp.where(core == 0, second, first)
+        first_core = place_ref[0] == 0
+        for y in range(CHUNKS // 2):
+            for part, pair in (
+                (slice(0, INNER), [total[:, LANES * m : LANES * m + LANES] for m in (2 * y, 2 * y + 1)]),
+                (slice(INNER, OUT_HEIGHT), [chunk_of(table, m, OUT_LANES) for m in (2 * y, 2 * y + 1)]),
+            ):
+                keep_ref[y, part, :] = jnp.where(first_core, pair[0], pair[1]).astype(BF)
+                send_ref[y, part, :] = jnp.where(first_core, pair[1], pair[0]).astype(BF)
 
 
 def output(place, mixed, x, out_grad, modulation, w_out, table):
-    half = jax.ShapeDtypeStruct((CHIPS, INNER // DP + 4, D), BF)
+    half = jax.ShapeDtypeStruct((CHUNKS // 2, OUT_HEIGHT, LANES), BF)
     return pl.pallas_call(
         output_kernel,
         grid=(POS // ROWS,),
@@ -319,7 +326,7 @@
             pl.BlockSpec(half.shape, lambda j: (0, 0, 0)),
         ],
         out_shape=[jax.ShapeDtypeStruct((POS, D), BF), half, half],
-        scratch_shapes=[pltpu.VMEM((INNER, D), F32), pltpu.VMEM((8, D), F32)],
+        scratch_shapes=[pltpu.VMEM((INNER, CHUNKS * LANES), F32), pltpu.VMEM((8, D), F32)],
         compiler_params=PARAMS,
         cost_estimate=pl.CostEstimate(
             flops=4 * POS * D * INNER, bytes_accessed=9_000_000, transcendentals=0
@@ -349,16 +356,14 @@
     total = refs[4]
     total[...] = (keep_ref[...].astype(F32) + got_ref[...].astype(F32)).astype(BF)
     for r in range(4):
-        y = lax.rem(place_ref[1] + r, 4)
-        for x in range(2):
-            refs[r][x] = total[2 * y + x]
+        refs[r][...] = total[lax.rem(place_ref[1] + r, 4)]
 
 
 def pair_turn(place, keep, got):
     return whole_call(
         pair_turn_kernel,
         "pair_turn",
-        [jax.ShapeDtypeStruct((2,) + keep.shape[1:], BF)] * 4,
+        [jax.ShapeDtypeStruct(keep.shape[1:], BF)] * 4,
         place,
         keep,
         got,
@@ -367,89 +372,56 @@
     )
 
 
-def stacked(block, rows):
-    height, width = block.shape
-    tiles = [block[:, c : c + 128] for c in range(0, width // 128 * 128, 128)]
-    if width % 128:
-        last = block[:, width // 128 * 128 :]
-        tiles.append(jnp.concatenate([last, jnp.zeros((height, 128 - width % 128), F32)], axis=1))
-    tiles.append(jnp.zeros((rows - height * len(tiles), 128), F32))
-    return jnp.concatenate(tiles, axis=0)
-
-
-def unstacked(rows, height, width):
-    tiles = [rows[height * c : height * c + height] for c in range(-(-width // 128))]
-    return jnp.concatenate(tiles, axis=1)[:, :width]
-
-
 def pieces_kernel(qkv_ref, o0, o1, o2, o3, pieces_ref):
-    parts = []
-    for x in range(2):
-        out = (o0[x].astype(F32) + o2[x].astype(F32)) + (o1[x].astype(F32) + o3[x].astype(F32))
-        parts.append(stacked(qkv_ref[x].astype(F32), SEQ * QKV_ROWS))
-        parts.append(stacked(out[: INNER // DP], SEQ * OUT_ROWS))
-    table = stacked(jnp.concatenate([out[INNER // DP :], jnp.zeros((4, D), F32)], axis=0)[:3], 32)
-    for s in range(SEQ):
-        rows = [p[h * s : h * s + h] for p, h in zip(parts, (QKV_ROWS, OUT_ROWS) * 2)]
-        rows += [table[2 * s : 2 * s + 2], jnp.zeros((6, 128), F32)]
-        pieces_ref[s] = jnp.concatenate(rows, axis=0).astype(BF)
-
-
-def block_pieces(qkv_blocks, out_blocks):
+    qkv = qkv_ref[0].astype(F32)
+    out = (o0[...].astype(F32) + o2[...].astype(F32)) + (o1[...].astype(F32) + o3[...].astype(F32))
+    table = out[INNER : INNER + 3]
+    rows, out_rows = D // SEQ, INNER // SEQ
+    for t in range(SEQ):
+        q = qkv[rows * t : rows * t + rows]
+        w = out[out_rows * t : out_rows * t + out_rows]
+        side = [w[:, 128:OUT_LANES], table[:, 128:OUT_LANES], jnp.zeros((33, 16), F32)]
+        right = [q[:, 128:QKV_LANES], jnp.concatenate(side, axis=0), jnp.zeros((rows, 24), F32)]
+        piece = [q[:, :128], jnp.concatenate(right, axis=1)]
+        piece += [w[:, :128], table[:, :128], jnp.zeros((1, 128), F32)]
+        pieces_ref[t] = jnp.concatenate(piece, axis=0).astype(BF)
+
+
+def block_pieces(qkv_chunk, out_chunks):
     return whole_call(
         pieces_kernel,
         "block_pieces",
-        jax.ShapeDtypeStruct((SEQ, 2 * BLOCK_ROWS + 8, 128), BF),
-        qkv_blocks,
-        *out_blocks,
-    )
-
-
-def seq_sum_kernel(factor, place_ref, pieces_ref, own_ref, other_ref):
-    total = sum(pieces_ref[k].astype(F32) for k in range(SEQ)) * factor
-    first, second = total[:BLOCK_ROWS], total[BLOCK_ROWS : 2 * BLOCK_ROWS]
-    table = total[2 * BLOCK_ROWS :]
-    own = jnp.where(place_ref[2] == 0, first, second)
-    other = jnp.where(place_ref[2] == 0, second, first)
-    own_ref[...] = jnp.concatenate([own, table], axis=0)
-    other_ref[...] = jnp.concatenate([other, table], axis=0)
-
-
-def seq_sum(place, pieces, factor):
+        jax.ShapeDtypeStruct((SEQ, PIECE_ROWS, 128), BF),
+        qkv_chunk,
+        *out_chunks,
+    )
+
+
+def seq_sum_kernel(factor, got_ref, pieces_ref):
+    piece = (sum(got_ref[k].astype(F32) for k in range(SEQ)) * factor).astype(BF)
+    for k in range(DP):
+        pieces_ref[k] = piece
+
+
+def seq_sum(got, factor):
     return whole_call(
         functools.partial(seq_sum_kernel, factor),
         "seq_sum",
-        [jax.ShapeDtypeStruct((BLOCK_ROWS + 8, 128), F32)] * 2,
-        place,
-        pieces,
-        smem=1,
-    )
-
-
-def last_sum_kernel(own_ref, other_ref, pieces_ref):
-    piece = (own_ref[...] + other_ref[...]).astype(BF)
-    for k in range(DP):
-        pieces_ref[k] = piece
-
-
-def last_sum(own, other):
-    return whole_call(
-        last_sum_kernel,
-        "last_sum",
-        jax.ShapeDtypeStruct((DP, BLOCK_ROWS + 8, 128), BF),
-        own,
-        other,
+        jax.ShapeDtypeStruct((DP, PIECE_ROWS, 128), BF),
+        got,
     )
 
 
 def assemble_kernel(pieces_ref, qkv_ref, out_ref, table_ref):
-    pieces = [pieces_ref[s].astype(F32) for s in range(DP)]
-    qkv = jnp.concatenate([p[:QKV_ROWS] for p in pieces], axis=0)
-    out = jnp.concatenate([p[QKV_ROWS:BLOCK_ROWS] for p in pieces], axis=0)
-    table = jnp.concatenate([p[BLOCK_ROWS : BLOCK_ROWS + 2] for p in pieces], axis=0)
-    qkv_ref[...] = unstacked(qkv, D // SEQ, 3 * INNER)
-    out_ref[...] = unstacked(out, INNER // SEQ, D)
-    table_ref[...] = unstacked(table, 3, D)
+    qkv, out, table = [], [], []
+    for m in range(CHUNKS):
+        p = pieces_ref[m].astype(F32) + pieces_ref[CHUNKS + m].astype(F32)
+        qkv += [p[0:72], p[72:144, 0:88]]
+        out += [p[144:180], p[72:108, 88:104]]
+        table += [p[180:183], p[108:111, 88:104]]
+    qkv_ref[...] = jnp.concatenate(qkv, axis=1)
+    out_ref[...] = jnp.concatenate(out, axis=1)
+    table_ref[...] = jnp.concatenate(table, axis=1)
 
 
 def assemble(pieces):
@@ -473,7 +445,7 @@
     tokens, grad_rows = clip_tokens[0, 0], out_grad[0, 0]
     modulation = mod_table + time_mod[0]
     dp_at = lax.axis_index("dp")
-    place = jnp.stack([dp_at % 2, dp_at // 2 % 4, dp_at // 8]).astype(jnp.int32)
+    place = jnp.stack([dp_at % 2, dp_at // 2 % 4]).astype(jnp.int32)
     w_turned = w_qkv.T
     x_pos = exchange(tokens.reshape(SEQ, HERE, D), "seq")
     grad_mixed = grad_mixed_rows(grad_rows, modulation, w_out)
@@ -497,12 +469,7 @@
     delta = exchange(delta_pos, "seq")
     pieces, delta = lax.optimization_barrier((block_pieces(qkv_blocks, out_blocks), delta))
     pieces = exchange(pieces, "seq")
-    own, other = seq_sum(place, pieces, 1.0 / math.sqrt(DP * SEQ * POS))
-    turn = [(i * SEQ + s, s * SEQ + i) for i in range(DP) for s in range(SEQ)]
-    turn_other = [(i * SEQ + s, s * SEQ + (i ^ 8)) for i in range(DP) for s in range(SEQ)]
-    own = lax.ppermute(own, ("dp", "seq"), turn)
-    other = lax.ppermute(other, ("dp", "seq"), turn_other)
-    pieces = exchange(last_sum(own, other), "dp")
+    pieces = exchange(seq_sum(pieces, 1.0 / math.sqrt(DP * SEQ * POS)), "dp")
     qkv_grad, out_weight_grad, table = assemble(pieces)
     grad_tokens = (grad_rows.astype(F32) + delta.reshape(POS, D).astype(F32)).astype(BF)
     return (

time: 238 us -> 234 us (0.983)
  starting transfers between devices: 59 us -> 47.7 us
  waiting for transfers between devices: 75 us -> 79.3 us
  Pallas kernels: 55.4 us -> 58.1 us
    ppermute x2 -> x0, starting transfers between devices: 9.26 us -> none  [the longest x1 6.99 us: body(): own = lax.ppermute(own, ('dp', 'seq'), turn)]
    ppermute x3, waiting for transfers between devices: 11.7 us -> 19 us  [body(): out_blocks[r] = lax.ppermute(out_blocks[r], 'dp', route)]
    reduce_scatter x1, waiting for transfers between devices: 8 us -> 3.34 us  [body(): lax.psum_scatter(qkv_blocks, 'dp', scatter_dimension=0, axis_index_groups...]
    all_to_all x5, waiting for transfers between devices: 50.4 us -> 54 us  [exchange(): lax.all_to_all(blocks, axis, 0, 0, axis_index_groups=groups, tiled=True)]
    ppermute x2 -> x0, waiting for transfers between devices: 2.84 us -> none  [the longest x1 2.82 us: body(): other = lax.ppermute(other, ('dp', 'seq'), turn_other)]
  transfers between devices with their start and end apart: 12 -> 10, of which waited for: 9 -> 7; matrix products, arithmetic and copies ran while one was open for 2% -> 2% of each run, Pallas kernels for 22% -> 24%
where the time goes in v4:
time: 234 us; the launch traced here: 233 us
  waiting for transfers between devices  79.3 us (34%)
  Pallas kernels  58.1 us (25%)
  starting transfers between devices  47.7 us (20%)
  blocking collectives  26.5 us (11%)
  between operations  14.2 us (6%)
  other arithmetic  4.3 us (2%)
  local copies, waits for them, and re-layouts  3.3 us (1%)
    all_to_all x5, waiting for transfers between devices, exchange(): lax.all_to_all(blocks, axis, 0, 0, axis_index_groups=groups, tiled=True)  54 us
    all_to_all x5, starting transfers between devices, exchange(): lax.all_to_all(blocks, axis, 0, 0, axis_index_groups=groups, tiled=True)  40.8 us
    all_to_all x1, blocking collectives, exchange(): lax.all_to_all(blocks, axis, 0, 0, axis_index_groups=groups, tiled=True)  26.5 us
    pallas_call x1, Pallas kernels, backward(): pl.pallas_call(backward_kernel, grid=(STEPS,), in_specs=[pl.BlockSpec((SE...  24 us
    ppermute x3, waiting for transfers between devices, body(): out_blocks[r] = lax.ppermute(out_blocks[r], 'dp', route)  19 us
    pallas_call x1, Pallas kernels, forward(): pl.pallas_call(forward_kernel, grid=(STEPS,), in_specs=[pl.BlockSpec((SEQ...  15.8 us
    pallas_call x1, Pallas kernels, output(): pl.pallas_call(output_kernel, grid=(POS // ROWS,), in_specs=[pl.BlockSpec...  9.89 us
    ppermute x3, starting transfers between devices, body(): out_blocks[r] = lax.ppermute(out_blocks[r], 'dp', route)  4.97 us
  transfers between devices with their start and end apart: 10, of which 7 were waited for; matrix products, arithmetic and copies ran while one was open for 2% of the time, Pallas kernels for 24%

profile of v4, /device:TPU:1, one launch (start us, length us, event | category | flops | bytes accessed | tf_op | source)
XLA Modules:
  0.0 233.4 jit_solution(10716558507927263829)
XLA Ops:
  7.2 0.0 copy-start.7
  7.2 0.0 copy-start.8
  7.2 10.2 %all-to-all-start = ((bf16[16,48,1152]{2,1,0:T(8,128)(2,1)}), bf16[16,48,1152]{2,1,0:T(8,128)(2,1)S(1)}, u32[]{:S(2)}, u32[]{:S(2)}) async-start(bf16[16,48,1152]{2,1,0:T(8,128)(2,1)} %bitcast.16), calls=%async_computation | async-start | bytes 3538944 | tf_op jit(solution)/shard_map/all_to_all | solution.py:441
  17.4 0.0 copy-done.7
  17.4 0.0 copy-done.8
  17.4 0.6 bitcast_add_fusion.mod_ref
  18.0 4.9 %grad_mixed.1 = bf16[768,576]{1,0:T(8,128)(2,1)} custom-call(bf16[768,1152]{1,0:T(8,128)(2,1)} %bitcast.13, f32[3,1152]{1,0:T(4,128)} %bitcast_add_fusion.mod_ref, bf16[576,1152]{1,0:T(8,128)(2,1)} %w_ref.3), custom_call_target="tpu_custom_call" | custom-call | flops 1019215872 | bytes 4000000 | tf_op jit(solution)/shard_map/grad_mixed/pallas_call | solution.py:153
  22.9 34.8 %all-to-all-done.x_ref = bf16[16,48,1152]{2,1,0:T(8,128)(2,1)S(1)} async-done(((bf16[16,48,1152]{2,1,0:T(8,128)(2,1)}), bf16[16,48,1152]{2,1,0:T(8,128)(2,1)S(1)}, u32[]{:S(2)}, u32[]{:S(2)}) %all-to-all-start) | async-done | bytes 1769504 | tf_op jit(solution)/shard_map/all_to_all | solution.py:441
  57.7 0.0 copy-start.4
  57.7 6.8 %all-to-all-start.1 = ((bf16[16,48,576]{2,1,0:T(8,128)(2,1)}), bf16[16,48,576]{2,1,0:T(8,128)(2,1)S(1)}, u32[]{:S(2)}, u32[]{:S(2)}) async-start(bf16[16,48,576]{2,1,0:T(8,128)(2,1)} %bitcast.15), calls=%async_computation.1 | async-start | bytes 1966080 | tf_op jit(solution)/shard_map/all_to_all | solution.py:441
  64.5 0.0 copy-done.4
  64.5 15.8 %forward.1 = (bf16[768,1728]{1,0:T(8,128)(2,1)}, bf16[16,48,576]{2,1,0:T(8,128)(2,1)}) custom-call(bf16[16,48,1152]{2,1,0:T(8,128)(2,1)} %copy-done.4, f32[3,1152]{1,0:T(4,128)} %bitcast_add_fusion.mod_ref, bf16[1728,1152]{1,0:T(8,128)(2,1)} %bitcast.19), custom_call_target="tpu_custom_call" | custom-call | flops 6115295232 | bytes 12000000 | tf_op jit(solution)/shard_map/forward/pallas_call | solution.py:123
  80.3 8.3 %all-to-all-done.1.gm_ref = bf16[16,48,576]{2,1,0:T(8,128)(2,1)S(1)} async-done(((bf16[16,48,576]{2,1,0:T(8,128)(2,1)}), bf16[16,48,576]{2,1,0:T(8,128)(2,1)S(1)}, u32[]{:S(2)}, u32[]{:S(2)}) %all-to-all-start.1) | async-done | bytes 884768 | tf_op jit(solution)/shard_map/all_to_all | solution.py:441
  88.5 0.0 copy-start.6
  88.5 6.2 %all-to-all-start.2 = ((bf16[16,48,576]{2,1,0:T(8,128)(2,1)}), bf16[16,48,576]{2,1,0:T(8,128)(2,1)S(1)}, u32[]{:S(2)}, u32[]{:S(2)}) async-start(bf16[16,48,576]{2,1,0:T(8,128)(2,1)} %get-tuple-element.26), calls=%async_computation.2 | async-start | bytes 1966080 | tf_op jit(solution)/shard_map/all_to_all | solution.py:441
  94.8 0.0 reduce-scatter.2.cloned.1.call-start
  94.8 0.0 copy-done.6
  94.8 24.0 %backward.1 = (bf16[16,48,1152]{2,1,0:T(8,128)(2,1)}, bf16[8,1152,256]{2,1,0:T(8,128)(2,1)}, f32[8,1152]{1,0:T(8,128)}) custom-call(bf16[16,48,1152]{2,1,0:T(8,128)(2,1)} %copy-done.4, bf16[16,48,576]{2,1,0:T(8,128)(2,1)} %copy-done.6, bf16[768,1728]{1,0:T(8,128)(2,1)} %get-tuple-element.24.packed_ref, f32[3,1152]{1,0:T(4,128)} %bitcast_add_fusion.mod_ref, ...), custom_call_target="tpu_custom_call" | custom-call | flops 12230590464 | bytes 20000000 | tf_op jit(solution)/shard_map/backward/pallas_call | solution.py:239
  118.8 0.0 all-to-all-done.2
  118.8 0.0 copy-start.5
  118.8 0.0 reduce-scatter.2.cloned.1.call-update
  118.8 0.9 copy-done.5
  119.8 7.6 %all-to-all-start.3 = ((bf16[16,48,1152]{2,1,0:T(8,128)(2,1)}), bf16[16,48,1152]{2,1,0:T(8,128)(2,1)}, u32[]{:S(2)}, u32[]{:S(2)}) async-start(bf16[16,48,1152]{2,1,0:T(8,128)(2,1)} %get-tuple-element.37), calls=%async_computation.4 | async-start | bytes 3538944 | tf_op jit(solution)/shard_map/all_to_all | solution.py:441
  127.4 0.6 pad_add_fusion.place_ref
  128.0 0.0 copy-start.2
  128.0 9.9 %output.1 = (bf16[768,1152]{1,0:T(8,128)(2,1)}, bf16[4,592,256]{2,1,0:T(8,128)(2,1)}, bf16[4,592,256]{2,1,0:T(8,128)(2,1)}) custom-call(s32[2]{0:T(128)} %pad_add_fusion.place_ref, bf16[768,576]{1,0:T(8,128)(2,1)} %bitcast.18, bf16[768,1152]{1,0:T(8,128)(2,1)} %bitcast.17, bf16[768,1152]{1,0:T(8,128)(2,1)} %bitcast.14, f32[3,1152]{1,0:T(4,128)} %bitcast_add_fusion.mod_ref, ...), custom_call_target="tpu_custom_call" | custom-call | flops 2038431744 | bytes 9000000 | tf_op jit(solution)/shard_map/output/pallas_call | solution.py:311
  137.9 1.8 collective-permute-start
  139.7 2.8 %collective-permute-done.got_ref = bf16[4,592,256]{2,1,0:T(8,128)(2,1)S(1)} collective-permute-done((bf16[4,592,256]{2,1,0:T(8,128)(2,1)}, bf16[4,592,256]{2,1,0:T(8,128)(2,1)S(1)}, u32[]{:S(2)}, u32[]{:S(2)}) %collective-permute-start) | collective-permute-done | bytes 1212448 | tf_op jit(solution)/shard_map/ppermute | solution.py:465
  142.5 0.0 copy-done.2
  142.5 0.0 copy-start
  142.5 1.3 copy-done
  143.8 1.3 pair_turn.1
  145.1 1.5 collective-permute-start.1
  146.6 2.4 %collective-permute-start.2 = (bf16[592,256]{1,0:T(8,128)(2,1)S(1)}, bf16[592,256]{1,0:T(8,128)(2,1)S(1)}, u32[]{:S(2)}, u32[]{:S(2)}) collective-permute-start(bf16[592,256]{1,0:T(8,128)(2,1)S(1)} %get-tuple-element.35), channel_id=1, source_target_pairs={{0,64},{16,80},{32,96},{48,112},{64,0},{80,16},{96,32},{112,48},{1... | collective-permute-start | bytes 909320 | tf_op jit(solution)/shard_map/ppermute | solution.py:468
  149.0 1.1 collective-permute-start.3
  150.1 8.4 %collective-permute-done.1.o1 = bf16[592,256]{1,0:T(8,128)(2,1)S(1)} collective-permute-done((bf16[592,256]{1,0:T(8,128)(2,1)S(1)}, bf16[592,256]{1,0:T(8,128)(2,1)S(1)}, u32[]{:S(2)}, u32[]{:S(2)}) %collective-permute-start.1) | collective-permute-done | bytes 303136 | tf_op jit(solution)/shard_map/ppermute | solution.py:468
  158.5 10.6 %collective-permute-done.2.o2 = bf16[592,256]{1,0:T(8,128)(2,1)S(1)} collective-permute-done((bf16[592,256]{1,0:T(8,128)(2,1)S(1)}, bf16[592,256]{1,0:T(8,128)(2,1)S(1)}, u32[]{:S(2)}, u32[]{:S(2)}) %collective-permute-start.2) | collective-permute-done | bytes 303136 | tf_op jit(solution)/shard_map/ppermute | solution.py:468
  169.1 0.0 collective-permute-done.3.o3
  169.1 3.3 %reduce-scatter.2.cloned.1.call-done.qkv_ref = bf16[1,1152,256]{2,1,0:T(8,128)(2,1)} async-done(((bf16[8,1152,256]{2,1,0:T(8,128)(2,1)}), bf16[1,1152,256]{2,1,0:T(8,128)(2,1)}) %reduce-scatter.2.cloned.1.call-update) | async-done | bytes 589840 | tf_op jit(solution)/shard_map/reduce_scatter | solution.py:458
  172.4 0.0 copy-start.1
  172.4 1.1 copy-done.1
  173.5 0.3 block_pieces.1
  173.8 0.0 all-to-all-done.3
  173.8 26.5 %all_to_all.30.got_ref = bf16[16,184,128]{2,1,0:T(8,128)(2,1)S(1)} all-to-all(bf16[16,184,128]{2,1,0:T(8,128)(2,1)S(1)} %block_pieces.1), channel_id=1, replica_groups=mesh['dp'=16,'seq'=16] {'seq'}, dimensions={0} | all-to-all | bytes 1507328 | tf_op jit(solution)/shard_map/all_to_all | solution.py:441
  200.3 0.0 copy-start.3
  200.3 1.0 seq_sum.1
  201.3 10.1 %all-to-all-start.5 = ((bf16[16,184,128]{2,1,0:T(8,128)(2,1)}), bf16[16,184,128]{2,1,0:T(8,128)(2,1)S(1)}, u32[]{:S(2)}, u32[]{:S(2)}) async-start(bf16[16,184,128]{2,1,0:T(8,128)(2,1)} %seq_sum.1), calls=%async_computation.6 | async-start | bytes 1507328 | tf_op jit(solution)/shard_map/all_to_all | solution.py:441
  211.4 0.0 copy-done.3
  211.4 3.1 %fusion = bf16[1,1,768,1152]{3,2,1,0:T(8,128)(2,1)} fusion(bf16[1,1,768,1152]{3,2,1,0:T(8,128)(2,1)} %bitcast.10, bf16[1,1,768,1152]{3,2,1,0:T(8,128)(2,1)S(1)} %copy-done.3), kind=kLoop, calls=%fused_computation.1 | loop fusion | flops 3538944 | bytes 5308416 | tf_op jit(solution)/shard_map/convert_element_type | solution.py:474
  214.5 10.9 %all-to-all-done.5.pieces_ref = bf16[16,184,128]{2,1,0:T(8,128)(2,1)S(1)} async-done(((bf16[16,184,128]{2,1,0:T(8,128)(2,1)}), bf16[16,184,128]{2,1,0:T(8,128)(2,1)S(1)}, u32[]{:S(2)}, u32[]{:S(2)}) %all-to-all-start.5) | async-done | bytes 753696 | tf_op jit(solution)/shard_map/all_to_all | solution.py:441
  225.5 1.1 assemble.1
Async XLA Ops:
  7.2 10.2 %copy-start.7 = (f32[3,1152]{1,0:T(4,128)S(1)}, f32[3,1152]{1,0:T(4,128)}, u32[]{:S(2)}) copy-start(f32[3,1152]{1,0:T(4,128)} %param.8) | copy-start | bytes 41476
  7.2 10.2 %copy-start.8 = (f32[1,3,1152]{2,0,1:T(1,128)S(1)}, f32[1,3,1152]{2,0,1:T(1,128)}, u32[]{:S(2)}) copy-start(f32[1,3,1152]{2,0,1:T(1,128)} %param.7) | copy-start | bytes 41476
  7.2 50.6 %all-to-all-start = ((bf16[16,48,1152]{2,1,0:T(8,128)(2,1)}), bf16[16,48,1152]{2,1,0:T(8,128)(2,1)S(1)}, u32[]{:S(2)}, u32[]{:S(2)}) async-start(bf16[16,48,1152]{2,1,0:T(8,128)(2,1)} %bitcast.16), calls=%async_computation | async-start | bytes 3538944 | tf_op jit(solution)/shard_map/all_to_all | solution.py:441
  57.7 6.8 %copy-start.4 = (bf16[16,48,1152]{2,1,0:T(8,128)(2,1)}, bf16[16,48,1152]{2,1,0:T(8,128)(2,1)S(1)}, u32[]{:S(2)}) copy-start(bf16[16,48,1152]{2,1,0:T(8,128)(2,1)S(1)} %all-to-all-done.x_ref) | copy-start | bytes 5308420
  57.7 30.8 %all-to-all-start.1 = ((bf16[16,48,576]{2,1,0:T(8,128)(2,1)}), bf16[16,48,576]{2,1,0:T(8,128)(2,1)S(1)}, u32[]{:S(2)}, u32[]{:S(2)}) async-start(bf16[16,48,576]{2,1,0:T(8,128)(2,1)} %bitcast.15), calls=%async_computation.1 | async-start | bytes 1966080 | tf_op jit(solution)/shard_map/all_to_all | solution.py:441
  88.5 6.3 %copy-start.6 = (bf16[16,48,576]{2,1,0:T(8,128)(2,1)}, bf16[16,48,576]{2,1,0:T(8,128)(2,1)S(1)}, u32[]{:S(2)}) copy-start(bf16[16,48,576]{2,1,0:T(8,128)(2,1)S(1)} %all-to-all-done.1.gm_ref) | copy-start | bytes 2654212
  88.5 30.3 %all-to-all-start.2 = ((bf16[16,48,576]{2,1,0:T(8,128)(2,1)}), bf16[16,48,576]{2,1,0:T(8,128)(2,1)S(1)}, u32[]{:S(2)}, u32[]{:S(2)}) async-start(bf16[16,48,576]{2,1,0:T(8,128)(2,1)} %get-tuple-element.26), calls=%async_computation.2 | async-start | bytes 1966080 | tf_op jit(solution)/shard_map/all_to_all | solution.py:441
  94.8 77.7 %reduce-scatter.2.cloned.1.call-start = ((), (), s32[]{:S(2)}) async-start(), calls=%async_computation.7 | async-start | bytes 5308416 | tf_op jit(solution)/shard_map/reduce_scatter | solution.py:458
  118.8 0.9 copy-start.5
  119.8 54.0 %all-to-all-start.3 = ((bf16[16,48,1152]{2,1,0:T(8,128)(2,1)}), bf16[16,48,1152]{2,1,0:T(8,128)(2,1)}, u32[]{:S(2)}, u32[]{:S(2)}) async-start(bf16[16,48,1152]{2,1,0:T(8,128)(2,1)} %get-tuple-element.37), calls=%async_computation.4 | async-start | bytes 3538944 | tf_op jit(solution)/shard_map/all_to_all | solution.py:441
  128.0 14.6 %copy-start.2 = (s32[2]{0:T(128)S(1)}, s32[2]{0:T(128)}, u32[]{:S(2)}) copy-start(s32[2]{0:T(128)} %pad_add_fusion.place_ref) | copy-start | bytes 28
  137.9 4.7 %collective-permute-start = (bf16[4,592,256]{2,1,0:T(8,128)(2,1)}, bf16[4,592,256]{2,1,0:T(8,128)(2,1)S(1)}, u32[]{:S(2)}, u32[]{:S(2)}) collective-permute-start(bf16[4,592,256]{2,1,0:T(8,128)(2,1)} %get-tuple-element.32), channel_id=1, source_target_pairs={{0,16},{16,0},{32,48},{48,32},{64,80},{80,64},{96,112},{112,96},{1... | collective-permute-start | bytes 3637256 | tf_op jit(solution)/shard_map/ppermute | solution.py:465
  142.5 1.3 copy-start
  145.1 13.4 %collective-permute-start.1 = (bf16[592,256]{1,0:T(8,128)(2,1)S(1)}, bf16[592,256]{1,0:T(8,128)(2,1)S(1)}, u32[]{:S(2)}, u32[]{:S(2)}) collective-permute-start(bf16[592,256]{1,0:T(8,128)(2,1)S(1)} %get-tuple-element.34), channel_id=1, source_target_pairs={{0,32},{16,48},{32,64},{48,80},{64,96},{80,112},{96,0},{112,16},{1... | collective-permute-start | bytes 909320 | tf_op jit(solution)/shard_map/ppermute | solution.py:468
  146.6 22.5 %collective-permute-start.2 = (bf16[592,256]{1,0:T(8,128)(2,1)S(1)}, bf16[592,256]{1,0:T(8,128)(2,1)S(1)}, u32[]{:S(2)}, u32[]{:S(2)}) collective-permute-start(bf16[592,256]{1,0:T(8,128)(2,1)S(1)} %get-tuple-element.35), channel_id=1, source_target_pairs={{0,64},{16,80},{32,96},{48,112},{64,0},{80,16},{96,32},{112,48},{1... | collective-permute-start | bytes 909320 | tf_op jit(solution)/shard_map/ppermute | solution.py:468
  149.0 20.1 %collective-permute-start.3 = (bf16[592,256]{1,0:T(8,128)(2,1)S(1)}, bf16[592,256]{1,0:T(8,128)(2,1)S(1)}, u32[]{:S(2)}, u32[]{:S(2)}) collective-permute-start(bf16[592,256]{1,0:T(8,128)(2,1)S(1)} %get-tuple-element.36), channel_id=1, source_target_pairs={{0,96},{16,112},{32,0},{48,16},{64,32},{80,48},{96,64},{112,80},{1... | collective-permute-start | bytes 909320 | tf_op jit(solution)/shard_map/ppermute | solution.py:468
  172.4 1.1 copy-start.1
  200.3 11.1 %copy-start.3 = (bf16[1,1,768,1152]{3,2,1,0:T(8,128)(2,1)S(1)}, bf16[1,1,768,1152]{3,2,1,0:T(8,128)(2,1)}, u32[]{:S(2)}) copy-start(bf16[1,1,768,1152]{3,2,1,0:T(8,128)(2,1)} %param.11) | copy-start | bytes 5308420
  201.3 24.2 %all-to-all-start.5 = ((bf16[16,184,128]{2,1,0:T(8,128)(2,1)}), bf16[16,184,128]{2,1,0:T(8,128)(2,1)S(1)}, u32[]{:S(2)}, u32[]{:S(2)}) async-start(bf16[16,184,128]{2,1,0:T(8,128)(2,1)} %seq_sum.1), calls=%async_computation.6 | async-start | bytes 1507328 | tf_op jit(solution)/shard_map/all_to_all | solution.py:441
Sparse Core Ops, SparseCore 0:
  119.0 53.4 reduce-scatter.1
